TPU v7x, 128 devices: a whole 4x4x4 slice. The times are simulated.
128 devices in a mesh: section: 2 (over core), expert: 16 (over y, x), dp: 4 (over z).
Axes of the slice: x: 4, y: 4, z: 4, core: 2. Of those that a mesh axis runs over, the one named last changes fastest.
Arguments:
- tokens: bfloat16 [4, 2048, 2048], P(None, ('expert', 'dp')), may hold values from -6 to 6
- routes: int32 [2, 4, 2048, 2], P('section', None, ('expert', 'dp')), may hold values from 0 to 15, all different within a row; in each aligned block of 32 rows (0 to 31, 32 to 63, ..., all dimensions but the last counted through in order) at most 5 rows name the same one
- gate_probs: float32 [2, 4, 2048, 2], P('section', None, ('expert', 'dp')), may hold values from 0.1 to 1
- w_gate: bfloat16 [2, 16, 2048, 640], P('section', 'expert'), may hold values from -0.125 to 0.125
- w_up: bfloat16 [2, 16, 2048, 640], P('section', 'expert'), may hold values from -0.125 to 0.125
- w_down: bfloat16 [2, 16, 640, 2048], P('section', 'expert'), may hold values from -0.25 to 0.25
- cotangent: bfloat16 [4, 2048, 2048], P(None, ('expert', 'dp')), may hold values from -0.29882812 to 0.29882812
Outputs:
- grad_gate: float32 [2, 16, 2048, 640], P('section', 'expert', 'dp')
- grad_up: float32 [2, 16, 2048, 640], P('section', 'expert', 'dp')
- grad_down: float32 [2, 16, 640, 2048], P('section', 'expert', None, 'dp')
Inputs may be any that keep to these rules, and one draw needn't show every extreme that they name: `routes`: in each micro-batch and layer, the 32 token rows of one device (aligned blocks) name each expert at most 5 times, a bound that some block reaches; the 2 experts of a token differ.
All inputs are finite; a program needn't handle non-finite values.
Results may differ from a plain program's by a relative error of at most 0.015.
Values may be sent and summed in bfloat16 or wider, within the bound.
A program may use at most 64 MiB of HBM per device.

v0:
```python
import jax
import jax.numpy as jnp
from jax import lax
from jax.sharding import PartitionSpec as P

epsilon = 1e-05
contract_rows = (((0,), (0,)), ((), ()))
contract_cols = (((1,), (1,)), ((), ()))


def shifted(value, axis, by):
    size = lax.axis_size(axis)
    pairs = [(i, i + by) for i in range(size) if 0 <= i + by < size]
    return lax.ppermute(value, axis, pairs)


def inverse_rms(values):
    return lax.rsqrt(jnp.mean(values * values, -1, keepdims=True) + epsilon)


def slot_selector(route_ids, experts, cap_slots):
    row_count, top_k = route_ids.shape
    flat_ids = route_ids.reshape(-1)
    one_hot = (flat_ids[:, None] == jnp.arange(experts, dtype=jnp.int32)[None, :]).astype(jnp.int32)
    earlier = jnp.cumsum(one_hot, 0) - one_hot
    slot_num = jnp.sum(earlier * one_hot, 1)
    target = (flat_ids * cap_slots + slot_num).reshape(row_count, top_k)
    columns = jnp.arange(experts * cap_slots, dtype=jnp.int32)
    return (target[:, :, None] == columns[None, None, :]).astype(jnp.bfloat16)


def keep_entry(store, value, position, is_live):
    previous = lax.dynamic_index_in_dim(store, position, 0, keepdims=False)
    return lax.dynamic_update_index_in_dim(store, jnp.where(is_live, value, previous), position, 0)


def shards(tokens, routes, gate_probs, w_gate, w_up, w_down, cotangent):
    micro_count, row_count, model_width = tokens.shape
    top_k = routes.shape[-1]
    experts = lax.axis_size("expert")
    sections = lax.axis_size("section")
    cap_slots = min(row_count, row_count * top_k // experts + 1)
    slot_rows = experts * cap_slots
    hidden = w_gate.shape[-1]
    section_pos = lax.axis_index("section")
    weight_gate = w_gate[0, 0]
    weight_up = w_up[0, 0]
    weight_down = w_down[0, 0]
    route_all = routes[0]
    prob_all = gate_probs[0]
    steps_total = micro_count + sections - 1

    def expert_forward(portion):
        leading = portion.shape[:-1]
        rows_flat = portion.reshape(-1, model_width)
        pre_gate = jnp.dot(rows_flat, weight_gate, preferred_element_type=jnp.float32)
        pre_up = jnp.dot(rows_flat, weight_up, preferred_element_type=jnp.float32)
        activation = (jax.nn.silu(pre_gate) * pre_up).astype(jnp.bfloat16)
        produced = jnp.dot(activation, weight_down, preferred_element_type=jnp.float32).astype(
            jnp.bfloat16
        )
        return (
            portion,
            pre_gate.reshape(leading + (hidden,)),
            pre_up.reshape(leading + (hidden,)),
            produced.reshape(portion.shape),
        )

    def forward_step(step_num, carried):
        incoming, keep_x, keep_rows, keep_gate, keep_up = carried
        micro_pos = step_num - section_pos
        is_live = (micro_pos >= 0) & (micro_pos < micro_count)
        position = jnp.clip(micro_pos, 0, micro_count - 1)
        fresh = lax.dynamic_index_in_dim(tokens, position, 0, keepdims=False)
        current = jnp.where(section_pos == 0, fresh, incoming)
        current_f = current.astype(jnp.float32)
        normed = (current_f * inverse_rms(current_f)).astype(jnp.bfloat16)
        route_ids = lax.dynamic_index_in_dim(route_all, position, 0, keepdims=False)
        probs = lax.dynamic_index_in_dim(prob_all, position, 0, keepdims=False)
        selector = slot_selector(route_ids, experts, cap_slots)
        outgoing = jnp.einsum(
            "rkj,rd->jd", selector, normed, preferred_element_type=jnp.float32
        ).astype(jnp.bfloat16)
        outgoing = outgoing.reshape(experts, cap_slots, model_width)
        received, pre_gate, pre_up, produced = expert_forward(
            lax.all_to_all(outgoing, "expert", split_axis=0, concat_axis=0, tiled=True)
        )
        returned = lax.all_to_all(produced, "expert", split_axis=0, concat_axis=0, tiled=True)
        chosen = jnp.einsum(
            "rkj,jd->rkd",
            selector,
            returned.reshape(slot_rows, model_width),
            preferred_element_type=jnp.float32,
        )
        mixed = (current_f + jnp.einsum("rk,rkd->rd", probs, chosen)).astype(jnp.bfloat16)
        keep_x = keep_entry(keep_x, current, position, is_live)
        keep_rows = keep_entry(
            keep_rows, received.reshape(slot_rows, model_width), position, is_live
        )
        keep_gate = keep_entry(keep_gate, pre_gate.reshape(slot_rows, hidden), position, is_live)
        keep_up = keep_entry(keep_up, pre_up.reshape(slot_rows, hidden), position, is_live)
        incoming = shifted(mixed, "section", 1)
        return (incoming, keep_x, keep_rows, keep_gate, keep_up)

    start_forward = (
        jnp.zeros((row_count, model_width), jnp.bfloat16),
        jnp.zeros((micro_count, row_count, model_width), jnp.bfloat16),
        jnp.zeros((micro_count, slot_rows, model_width), jnp.bfloat16),
        jnp.zeros((micro_count, slot_rows, hidden), jnp.float32),
        jnp.zeros((micro_count, slot_rows, hidden), jnp.float32),
    )
    finished = lax.fori_loop(0, steps_total, forward_step, start_forward)
    keep_x, keep_rows, keep_gate, keep_up = (finished[1], finished[2], finished[3], finished[4])

    def local_backward(operands):
        arrived, pre_gate, pre_up = operands
        back_hidden = lax.dot_general(
            arrived, weight_down, contract_cols, preferred_element_type=jnp.float32
        )
        sigmoid_gate = jax.nn.sigmoid(pre_gate)
        silu_gate = pre_gate * sigmoid_gate
        d_gate = (
            back_hidden * pre_up * sigmoid_gate * (1.0 + pre_gate * (1.0 - sigmoid_gate))
        ).astype(jnp.bfloat16)
        d_up = (back_hidden * silu_gate).astype(jnp.bfloat16)
        activation = (silu_gate * pre_up).astype(jnp.bfloat16)
        d_rows = (
            lax.dot_general(d_gate, weight_gate, contract_cols, preferred_element_type=jnp.float32)
            + lax.dot_general(d_up, weight_up, contract_cols, preferred_element_type=jnp.float32)
        ).astype(jnp.bfloat16)
        return (d_gate, d_up, activation, d_rows)

    def backward_step(step_num, carried):
        incoming, keep_go, keep_dgate, keep_dup, keep_act = carried
        micro_pos = step_num - (sections - 1 - section_pos)
        is_live = (micro_pos >= 0) & (micro_pos < micro_count)
        position = jnp.clip(micro_pos, 0, micro_count - 1)
        given_grad = lax.dynamic_index_in_dim(cotangent, position, 0, keepdims=False)
        upstream = jnp.where(section_pos == sections - 1, given_grad, incoming)
        upstream = jnp.where(is_live, upstream, jnp.zeros_like(upstream))
        upstream_f = upstream.astype(jnp.float32)
        current_f = lax.dynamic_index_in_dim(keep_x, position, 0, keepdims=False).astype(
            jnp.float32
        )
        route_ids = lax.dynamic_index_in_dim(route_all, position, 0, keepdims=False)
        probs = lax.dynamic_index_in_dim(prob_all, position, 0, keepdims=False)
        selector = slot_selector(route_ids, experts, cap_slots)
        scaled = (probs[:, :, None] * upstream_f[:, None, :]).astype(jnp.bfloat16)
        outgoing = jnp.einsum(
            "rkj,rkd->jd", selector, scaled, preferred_element_type=jnp.float32
        ).astype(jnp.bfloat16)
        arrived = lax.all_to_all(
            outgoing.reshape(experts, cap_slots, model_width),
            "expert",
            split_axis=0,
            concat_axis=0,
            tiled=True,
        )
        arrived = arrived.reshape(slot_rows, model_width)
        pre_gate = lax.dynamic_index_in_dim(keep_gate, position, 0, keepdims=False)
        pre_up = lax.dynamic_index_in_dim(keep_up, position, 0, keepdims=False)
        d_gate, d_up, activation, d_rows = local_backward((arrived, pre_gate, pre_up))
        sent_back = lax.all_to_all(
            d_rows.reshape(experts, cap_slots, model_width),
            "expert",
            split_axis=0,
            concat_axis=0,
            tiled=True,
        )
        d_normed = jnp.einsum(
            "rkj,jd->rd",
            selector,
            sent_back.reshape(slot_rows, model_width),
            preferred_element_type=jnp.float32,
        )
        scale_rms = inverse_rms(current_f)
        d_current = scale_rms * d_normed - current_f * scale_rms**3 * jnp.mean(
            d_normed * current_f, -1, keepdims=True
        )
        passed = (upstream_f + d_current).astype(jnp.bfloat16)
        keep_go = keep_entry(keep_go, arrived, position, is_live)
        keep_dgate = keep_entry(keep_dgate, d_gate, position, is_live)
        keep_dup = keep_entry(keep_dup, d_up, position, is_live)
        keep_act = keep_entry(keep_act, activation, position, is_live)
        incoming = shifted(passed, "section", -1)
        return (incoming, keep_go, keep_dgate, keep_dup, keep_act)

    start_backward = (
        jnp.zeros((row_count, model_width), jnp.bfloat16),
        jnp.zeros((micro_count, slot_rows, model_width), jnp.bfloat16),
        jnp.zeros((micro_count, slot_rows, hidden), jnp.bfloat16),
        jnp.zeros((micro_count, slot_rows, hidden), jnp.bfloat16),
        jnp.zeros((micro_count, slot_rows, hidden), jnp.bfloat16),
    )
    done = lax.fori_loop(0, steps_total, backward_step, start_backward)
    all_rows = micro_count * slot_rows
    rows_all = keep_rows.reshape(all_rows, model_width)
    go_all = done[1].reshape(all_rows, model_width)
    dgate_all = done[2].reshape(all_rows, hidden)
    dup_all = done[3].reshape(all_rows, hidden)
    act_all = done[4].reshape(all_rows, hidden)
    local_gate = lax.dot_general(
        rows_all, dgate_all, contract_rows, preferred_element_type=jnp.float32
    )
    local_up = lax.dot_general(rows_all, dup_all, contract_rows, preferred_element_type=jnp.float32)
    local_down = lax.dot_general(act_all, go_all, contract_rows, preferred_element_type=jnp.float32)
    grad_gate, grad_up, grad_down = (
        lax.psum_scatter(
            local_gate.astype(jnp.bfloat16), "dp", scatter_dimension=0, tiled=True
        ).astype(jnp.float32),
        lax.psum_scatter(
            local_up.astype(jnp.bfloat16), "dp", scatter_dimension=0, tiled=True
        ).astype(jnp.float32),
        lax.psum_scatter(
            local_down.astype(jnp.bfloat16), "dp", scatter_dimension=1, tiled=True
        ).astype(jnp.float32),
    )
    return (grad_gate[None, None], grad_up[None, None], grad_down[None, None])


def solution(mesh):
    in_specs = (
        P(None, ("expert", "dp"), None),
        P("section", None, ("expert", "dp"), None),
        P("section", None, ("expert", "dp"), None),
        P("section", "expert", None, None),
        P("section", "expert", None, None),
        P("section", "expert", None, None),
        P(None, ("expert", "dp"), None),
    )
    out_specs = (
        P("section", "expert", "dp", None),
        P("section", "expert", "dp", None),
        P("section", "expert", None, "dp"),
    )
    return jax.shard_map(shards, mesh=mesh, in_specs=in_specs, out_specs=out_specs, check_vma=False)
```

profile of v0, /device:TPU:0, one launch (start us, length us, event | category | flops | bytes accessed | tf_op | source)
XLA Modules:
  0.0 648.5 jit_solution(1374725079667835370)
XLA Ops:
  12.7 251.2 %while.45 = (s32[]{:T(128)}, bf16[32,2048]{1,0:T(8,128)(2,1)}, bf16[4,32,2048]{2,1,0:T(8,128)(2,1)}, bf16[4,80,2048]{2,1,0:T(8,128)(2,1)}, f32[4,80,640]{2,1,0:T...) while((s32[]{:T(128)}, bf16[32,2048]{1,0:T(8,128)(2,1)}, ...), condition=%wide.region_5.6_spmd, body=%wide.region_0.5_spmd.sunk | while | flops 662418048 | bytes 46170776 | solution.py:112
  26.9 9.8 %all-to-all-done = bf16[16,5,2048]{2,1,0:T(8,128)(2,1)S(1)} async-done(((bf16[16,5,2048]{2,1,0:T(8,128)(2,1)}), bf16[16,5,2048]{2,1,0:T(8,128)(2,1)S(1)}, u32[]{:S(2)}, u32[]{:S(2)}) %all-to-all-start) | async-done | bytes 327712 | tf_op jit(solution)/shard_map/while/body/eval_jaxpr/all_to_all | solution.py:86
  49.6 9.5 %all-to-all-done.1 = bf16[16,5,2048]{2,1,0:T(8,128)(2,1)} async-done(((bf16[16,5,2048]{2,1,0:T(8,128)(2,1)}), bf16[16,5,2048]{2,1,0:T(8,128)(2,1)}, u32[]{:S(2)}, u32[]{:S(2)}) %all-to-all-start.1) | async-done | bytes 327712 | tf_op jit(solution)/shard_map/while/body/eval_jaxpr/all_to_all | solution.py:88
  77.2 9.2 %all-to-all-done = bf16[16,5,2048]{2,1,0:T(8,128)(2,1)S(1)} async-done(((bf16[16,5,2048]{2,1,0:T(8,128)(2,1)}), bf16[16,5,2048]{2,1,0:T(8,128)(2,1)S(1)}, u32[]{:S(2)}, u32[]{:S(2)}) %all-to-all-start) | async-done | bytes 327712 | tf_op jit(solution)/shard_map/while/body/eval_jaxpr/all_to_all | solution.py:86
  99.2 9.2 %all-to-all-done.1 = bf16[16,5,2048]{2,1,0:T(8,128)(2,1)} async-done(((bf16[16,5,2048]{2,1,0:T(8,128)(2,1)}), bf16[16,5,2048]{2,1,0:T(8,128)(2,1)}, u32[]{:S(2)}, u32[]{:S(2)}) %all-to-all-start.1) | async-done | bytes 327712 | tf_op jit(solution)/shard_map/while/body/eval_jaxpr/all_to_all | solution.py:88
  126.5 9.2 %all-to-all-done = bf16[16,5,2048]{2,1,0:T(8,128)(2,1)S(1)} async-done(((bf16[16,5,2048]{2,1,0:T(8,128)(2,1)}), bf16[16,5,2048]{2,1,0:T(8,128)(2,1)S(1)}, u32[]{:S(2)}, u32[]{:S(2)}) %all-to-all-start) | async-done | bytes 327712 | tf_op jit(solution)/shard_map/while/body/eval_jaxpr/all_to_all | solution.py:86
  148.6 9.2 %all-to-all-done.1 = bf16[16,5,2048]{2,1,0:T(8,128)(2,1)} async-done(((bf16[16,5,2048]{2,1,0:T(8,128)(2,1)}), bf16[16,5,2048]{2,1,0:T(8,128)(2,1)}, u32[]{:S(2)}, u32[]{:S(2)}) %all-to-all-start.1) | async-done | bytes 327712 | tf_op jit(solution)/shard_map/while/body/eval_jaxpr/all_to_all | solution.py:88
  175.9 9.2 %all-to-all-done = bf16[16,5,2048]{2,1,0:T(8,128)(2,1)S(1)} async-done(((bf16[16,5,2048]{2,1,0:T(8,128)(2,1)}), bf16[16,5,2048]{2,1,0:T(8,128)(2,1)S(1)}, u32[]{:S(2)}, u32[]{:S(2)}) %all-to-all-start) | async-done | bytes 327712 | tf_op jit(solution)/shard_map/while/body/eval_jaxpr/all_to_all | solution.py:86
  198.0 9.2 %all-to-all-done.1 = bf16[16,5,2048]{2,1,0:T(8,128)(2,1)} async-done(((bf16[16,5,2048]{2,1,0:T(8,128)(2,1)}), bf16[16,5,2048]{2,1,0:T(8,128)(2,1)}, u32[]{:S(2)}, u32[]{:S(2)}) %all-to-all-start.1) | async-done | bytes 327712 | tf_op jit(solution)/shard_map/while/body/eval_jaxpr/all_to_all | solution.py:88
  225.3 9.2 %all-to-all-done = bf16[16,5,2048]{2,1,0:T(8,128)(2,1)S(1)} async-done(((bf16[16,5,2048]{2,1,0:T(8,128)(2,1)}), bf16[16,5,2048]{2,1,0:T(8,128)(2,1)S(1)}, u32[]{:S(2)}, u32[]{:S(2)}) %all-to-all-start) | async-done | bytes 327712 | tf_op jit(solution)/shard_map/while/body/eval_jaxpr/all_to_all | solution.py:86
  247.3 9.2 %all-to-all-done.1 = bf16[16,5,2048]{2,1,0:T(8,128)(2,1)} async-done(((bf16[16,5,2048]{2,1,0:T(8,128)(2,1)}), bf16[16,5,2048]{2,1,0:T(8,128)(2,1)}, u32[]{:S(2)}, u32[]{:S(2)}) %all-to-all-start.1) | async-done | bytes 327712 | tf_op jit(solution)/shard_map/while/body/eval_jaxpr/all_to_all | solution.py:88
  267.6 261.7 %while.46 = (s32[]{:T(128)}, bf16[32,2048]{1,0:T(8,128)(2,1)S(1)}, bf16[4,80,2048]{2,1,0:T(8,128)(2,1)}, bf16[4,80,640]{2,1,0:T(8,128)(2,1)}, bf16[4,80,640]{2,1...) while((s32[]{:T(128)}, bf16[32,2048]{1,0:T(8,128)(2,1)S(1)}, ...), condition=%wide.region_12.13_spmd, body=%wide.region_6.12_spmd.sunk | while | flops 663724672 | bytes 32352672 | solution.py:195
  276.4 9.3 %all-to-all-done.2 = bf16[16,5,2048]{2,1,0:T(8,128)(2,1)S(1)} async-done(((bf16[16,5,2048]{2,1,0:T(8,128)(2,1)}), bf16[16,5,2048]{2,1,0:T(8,128)(2,1)S(1)}, u32[]{:S(2)}, u32[]{:S(2)}) %all-to-all-start.2) | async-done | bytes 327712 | tf_op jit(solution)/shard_map/while/body/eval_jaxpr/all_to_all | solution.py:152
  325.5 11.5 %all-to-all-done.2 = bf16[16,5,2048]{2,1,0:T(8,128)(2,1)S(1)} async-done(((bf16[16,5,2048]{2,1,0:T(8,128)(2,1)}), bf16[16,5,2048]{2,1,0:T(8,128)(2,1)S(1)}, u32[]{:S(2)}, u32[]{:S(2)}) %all-to-all-start.2) | async-done | bytes 327712 | tf_op jit(solution)/shard_map/while/body/eval_jaxpr/all_to_all | solution.py:152
  351.9 11.1 %all-to-all-done.3 = bf16[16,5,2048]{2,1,0:T(8,128)(2,1)} async-done(((bf16[16,5,2048]{2,1,0:T(8,128)(2,1)}), bf16[16,5,2048]{2,1,0:T(8,128)(2,1)}, u32[]{:S(2)}, u32[]{:S(2)}) %all-to-all-start.3) | async-done | bytes 327712 | tf_op jit(solution)/shard_map/while/body/eval_jaxpr/all_to_all | solution.py:163
  378.6 11.5 %all-to-all-done.2 = bf16[16,5,2048]{2,1,0:T(8,128)(2,1)S(1)} async-done(((bf16[16,5,2048]{2,1,0:T(8,128)(2,1)}), bf16[16,5,2048]{2,1,0:T(8,128)(2,1)S(1)}, u32[]{:S(2)}, u32[]{:S(2)}) %all-to-all-start.2) | async-done | bytes 327712 | tf_op jit(solution)/shard_map/while/body/eval_jaxpr/all_to_all | solution.py:152
  405.1 11.1 %all-to-all-done.3 = bf16[16,5,2048]{2,1,0:T(8,128)(2,1)} async-done(((bf16[16,5,2048]{2,1,0:T(8,128)(2,1)}), bf16[16,5,2048]{2,1,0:T(8,128)(2,1)}, u32[]{:S(2)}, u32[]{:S(2)}) %all-to-all-start.3) | async-done | bytes 327712 | tf_op jit(solution)/shard_map/while/body/eval_jaxpr/all_to_all | solution.py:163
  431.8 11.5 %all-to-all-done.2 = bf16[16,5,2048]{2,1,0:T(8,128)(2,1)S(1)} async-done(((bf16[16,5,2048]{2,1,0:T(8,128)(2,1)}), bf16[16,5,2048]{2,1,0:T(8,128)(2,1)S(1)}, u32[]{:S(2)}, u32[]{:S(2)}) %all-to-all-start.2) | async-done | bytes 327712 | tf_op jit(solution)/shard_map/while/body/eval_jaxpr/all_to_all | solution.py:152
  458.2 11.1 %all-to-all-done.3 = bf16[16,5,2048]{2,1,0:T(8,128)(2,1)} async-done(((bf16[16,5,2048]{2,1,0:T(8,128)(2,1)}), bf16[16,5,2048]{2,1,0:T(8,128)(2,1)}, u32[]{:S(2)}, u32[]{:S(2)}) %all-to-all-start.3) | async-done | bytes 327712 | tf_op jit(solution)/shard_map/while/body/eval_jaxpr/all_to_all | solution.py:163
  485.0 11.5 %all-to-all-done.2 = bf16[16,5,2048]{2,1,0:T(8,128)(2,1)S(1)} async-done(((bf16[16,5,2048]{2,1,0:T(8,128)(2,1)}), bf16[16,5,2048]{2,1,0:T(8,128)(2,1)S(1)}, u32[]{:S(2)}, u32[]{:S(2)}) %all-to-all-start.2) | async-done | bytes 327712 | tf_op jit(solution)/shard_map/while/body/eval_jaxpr/all_to_all | solution.py:152
  511.4 11.1 %all-to-all-done.3 = bf16[16,5,2048]{2,1,0:T(8,128)(2,1)} async-done(((bf16[16,5,2048]{2,1,0:T(8,128)(2,1)}), bf16[16,5,2048]{2,1,0:T(8,128)(2,1)}, u32[]{:S(2)}, u32[]{:S(2)}) %all-to-all-start.3) | async-done | bytes 327712 | tf_op jit(solution)/shard_map/while/body/eval_jaxpr/all_to_all | solution.py:163
  543.0 24.2 %reduce-scatter.6.cloned.1.call-done = bf16[512,640]{1,0:T(8,128)(2,1)} async-done(((bf16[2048,640]{1,0:T(8,128)(2,1)}), bf16[512,640]{1,0:T(8,128)(2,1)}) %reduce-scatter.6.cloned.1.call-update) | async-done | bytes 655376 | tf_op jit(solution)/shard_map/reduce_scatter | solution.py:211
  569.4 34.0 %reduce-scatter.4.cloned.1.call-done = bf16[512,640]{1,0:T(8,128)(2,1)} async-done(((bf16[2048,640]{1,0:T(8,128)(2,1)}), bf16[512,640]{1,0:T(8,128)(2,1)}) %reduce-scatter.4.cloned.1.call-update) | async-done | bytes 655376 | tf_op jit(solution)/shard_map/reduce_scatter | solution.py:208
  605.6 34.0 %reduce-scatter.8.cloned.1.call-done = bf16[640,512]{1,0:T(8,128)(2,1)} async-done(((bf16[640,2048]{1,0:T(8,128)(2,1)}), bf16[640,512]{1,0:T(8,128)(2,1)}) %reduce-scatter.8.cloned.1.call-update) | async-done | bytes 655376 | tf_op jit(solution)/shard_map/reduce_scatter | solution.py:214
  (431 shorter events, 348.7 us)
Async XLA Ops:
  7.2 560.0 %reduce-scatter.6.cloned.1.call-start = ((), (), s32[]{:S(2)}) async-start(), calls=%async_computation.8 | async-start | bytes 3276800 | tf_op jit(solution)/shard_map/reduce_scatter | solution.py:211
  18.0 18.7 %all-to-all-start = ((bf16[16,5,2048]{2,1,0:T(8,128)(2,1)}), bf16[16,5,2048]{2,1,0:T(8,128)(2,1)S(1)}, u32[]{:S(2)}, u32[]{:S(2)}) async-start(bf16[16,5,2048]{2,1,0:T(8,128)(2,1)} %reshape.220), calls=%async_computation | async-start | bytes 1048576 | tf_op jit(solution)/shard_map/while/body/eval_jaxpr/all_to_all | solution.py:86
  44.3 14.7 %all-to-all-start.1 = ((bf16[16,5,2048]{2,1,0:T(8,128)(2,1)}), bf16[16,5,2048]{2,1,0:T(8,128)(2,1)}, u32[]{:S(2)}, u32[]{:S(2)}) async-start(bf16[16,5,2048]{2,1,0:T(8,128)(2,1)} %reshape.222), calls=%async_computation.1 | async-start | bytes 1048576 | tf_op jit(solution)/shard_map/while/body/eval_jaxpr/all_to_all | solution.py:88
  71.7 14.6 %all-to-all-start = ((bf16[16,5,2048]{2,1,0:T(8,128)(2,1)}), bf16[16,5,2048]{2,1,0:T(8,128)(2,1)S(1)}, u32[]{:S(2)}, u32[]{:S(2)}) async-start(bf16[16,5,2048]{2,1,0:T(8,128)(2,1)} %reshape.220), calls=%async_computation | async-start | bytes 1048576 | tf_op jit(solution)/shard_map/while/body/eval_jaxpr/all_to_all | solution.py:86
  93.9 14.5 %all-to-all-start.1 = ((bf16[16,5,2048]{2,1,0:T(8,128)(2,1)}), bf16[16,5,2048]{2,1,0:T(8,128)(2,1)}, u32[]{:S(2)}, u32[]{:S(2)}) async-start(bf16[16,5,2048]{2,1,0:T(8,128)(2,1)} %reshape.222), calls=%async_computation.1 | async-start | bytes 1048576 | tf_op jit(solution)/shard_map/while/body/eval_jaxpr/all_to_all | solution.py:88
  112.1 3.7 collective-permute-start
  121.1 14.6 %all-to-all-start = ((bf16[16,5,2048]{2,1,0:T(8,128)(2,1)}), bf16[16,5,2048]{2,1,0:T(8,128)(2,1)S(1)}, u32[]{:S(2)}, u32[]{:S(2)}) async-start(bf16[16,5,2048]{2,1,0:T(8,128)(2,1)} %reshape.220), calls=%async_computation | async-start | bytes 1048576 | tf_op jit(solution)/shard_map/while/body/eval_jaxpr/all_to_all | solution.py:86
  143.3 14.5 %all-to-all-start.1 = ((bf16[16,5,2048]{2,1,0:T(8,128)(2,1)}), bf16[16,5,2048]{2,1,0:T(8,128)(2,1)}, u32[]{:S(2)}, u32[]{:S(2)}) async-start(bf16[16,5,2048]{2,1,0:T(8,128)(2,1)} %reshape.222), calls=%async_computation.1 | async-start | bytes 1048576 | tf_op jit(solution)/shard_map/while/body/eval_jaxpr/all_to_all | solution.py:88
  170.5 14.6 %all-to-all-start = ((bf16[16,5,2048]{2,1,0:T(8,128)(2,1)}), bf16[16,5,2048]{2,1,0:T(8,128)(2,1)S(1)}, u32[]{:S(2)}, u32[]{:S(2)}) async-start(bf16[16,5,2048]{2,1,0:T(8,128)(2,1)} %reshape.220), calls=%async_computation | async-start | bytes 1048576 | tf_op jit(solution)/shard_map/while/body/eval_jaxpr/all_to_all | solution.py:86
  192.7 14.5 %all-to-all-start.1 = ((bf16[16,5,2048]{2,1,0:T(8,128)(2,1)}), bf16[16,5,2048]{2,1,0:T(8,128)(2,1)}, u32[]{:S(2)}, u32[]{:S(2)}) async-start(bf16[16,5,2048]{2,1,0:T(8,128)(2,1)} %reshape.222), calls=%async_computation.1 | async-start | bytes 1048576 | tf_op jit(solution)/shard_map/while/body/eval_jaxpr/all_to_all | solution.py:88
  219.9 14.6 %all-to-all-start = ((bf16[16,5,2048]{2,1,0:T(8,128)(2,1)}), bf16[16,5,2048]{2,1,0:T(8,128)(2,1)S(1)}, u32[]{:S(2)}, u32[]{:S(2)}) async-start(bf16[16,5,2048]{2,1,0:T(8,128)(2,1)} %reshape.220), calls=%async_computation | async-start | bytes 1048576 | tf_op jit(solution)/shard_map/while/body/eval_jaxpr/all_to_all | solution.py:86
  242.1 14.5 %all-to-all-start.1 = ((bf16[16,5,2048]{2,1,0:T(8,128)(2,1)}), bf16[16,5,2048]{2,1,0:T(8,128)(2,1)}, u32[]{:S(2)}, u32[]{:S(2)}) async-start(bf16[16,5,2048]{2,1,0:T(8,128)(2,1)} %reshape.222), calls=%async_computation.1 | async-start | bytes 1048576 | tf_op jit(solution)/shard_map/while/body/eval_jaxpr/all_to_all | solution.py:88
  271.2 14.5 %all-to-all-start.2 = ((bf16[16,5,2048]{2,1,0:T(8,128)(2,1)}), bf16[16,5,2048]{2,1,0:T(8,128)(2,1)S(1)}, u32[]{:S(2)}, u32[]{:S(2)}) async-start(bf16[16,5,2048]{2,1,0:T(8,128)(2,1)} %reshape.225), calls=%async_computation.2 | async-start | bytes 1048576 | tf_op jit(solution)/shard_map/while/body/eval_jaxpr/all_to_all | solution.py:152
  295.5 14.4 %all-to-all-start.3 = ((bf16[16,5,2048]{2,1,0:T(8,128)(2,1)}), bf16[16,5,2048]{2,1,0:T(8,128)(2,1)}, u32[]{:S(2)}, u32[]{:S(2)}) async-start(bf16[16,5,2048]{2,1,0:T(8,128)(2,1)} %reshape.227), calls=%async_computation.3 | async-start | bytes 1048576 | tf_op jit(solution)/shard_map/while/body/eval_jaxpr/all_to_all | solution.py:163
  320.3 16.7 %all-to-all-start.2 = ((bf16[16,5,2048]{2,1,0:T(8,128)(2,1)}), bf16[16,5,2048]{2,1,0:T(8,128)(2,1)S(1)}, u32[]{:S(2)}, u32[]{:S(2)}) async-start(bf16[16,5,2048]{2,1,0:T(8,128)(2,1)} %reshape.225), calls=%async_computation.2 | async-start | bytes 1048576 | tf_op jit(solution)/shard_map/while/body/eval_jaxpr/all_to_all | solution.py:152
  346.7 16.4 %all-to-all-start.3 = ((bf16[16,5,2048]{2,1,0:T(8,128)(2,1)}), bf16[16,5,2048]{2,1,0:T(8,128)(2,1)}, u32[]{:S(2)}, u32[]{:S(2)}) async-start(bf16[16,5,2048]{2,1,0:T(8,128)(2,1)} %reshape.227), calls=%async_computation.3 | async-start | bytes 1048576 | tf_op jit(solution)/shard_map/while/body/eval_jaxpr/all_to_all | solution.py:163
  373.4 16.7 %all-to-all-start.2 = ((bf16[16,5,2048]{2,1,0:T(8,128)(2,1)}), bf16[16,5,2048]{2,1,0:T(8,128)(2,1)S(1)}, u32[]{:S(2)}, u32[]{:S(2)}) async-start(bf16[16,5,2048]{2,1,0:T(8,128)(2,1)} %reshape.225), calls=%async_computation.2 | async-start | bytes 1048576 | tf_op jit(solution)/shard_map/while/body/eval_jaxpr/all_to_all | solution.py:152
  399.9 16.4 %all-to-all-start.3 = ((bf16[16,5,2048]{2,1,0:T(8,128)(2,1)}), bf16[16,5,2048]{2,1,0:T(8,128)(2,1)}, u32[]{:S(2)}, u32[]{:S(2)}) async-start(bf16[16,5,2048]{2,1,0:T(8,128)(2,1)} %reshape.227), calls=%async_computation.3 | async-start | bytes 1048576 | tf_op jit(solution)/shard_map/while/body/eval_jaxpr/all_to_all | solution.py:163
  426.6 16.7 %all-to-all-start.2 = ((bf16[16,5,2048]{2,1,0:T(8,128)(2,1)}), bf16[16,5,2048]{2,1,0:T(8,128)(2,1)S(1)}, u32[]{:S(2)}, u32[]{:S(2)}) async-start(bf16[16,5,2048]{2,1,0:T(8,128)(2,1)} %reshape.225), calls=%async_computation.2 | async-start | bytes 1048576 | tf_op jit(solution)/shard_map/while/body/eval_jaxpr/all_to_all | solution.py:152
  453.0 16.4 %all-to-all-start.3 = ((bf16[16,5,2048]{2,1,0:T(8,128)(2,1)}), bf16[16,5,2048]{2,1,0:T(8,128)(2,1)}, u32[]{:S(2)}, u32[]{:S(2)}) async-start(bf16[16,5,2048]{2,1,0:T(8,128)(2,1)} %reshape.227), calls=%async_computation.3 | async-start | bytes 1048576 | tf_op jit(solution)/shard_map/while/body/eval_jaxpr/all_to_all | solution.py:163
  479.7 16.7 %all-to-all-start.2 = ((bf16[16,5,2048]{2,1,0:T(8,128)(2,1)}), bf16[16,5,2048]{2,1,0:T(8,128)(2,1)S(1)}, u32[]{:S(2)}, u32[]{:S(2)}) async-start(bf16[16,5,2048]{2,1,0:T(8,128)(2,1)} %reshape.225), calls=%async_computation.2 | async-start | bytes 1048576 | tf_op jit(solution)/shard_map/while/body/eval_jaxpr/all_to_all | solution.py:152
  506.2 16.4 %all-to-all-start.3 = ((bf16[16,5,2048]{2,1,0:T(8,128)(2,1)}), bf16[16,5,2048]{2,1,0:T(8,128)(2,1)}, u32[]{:S(2)}, u32[]{:S(2)}) async-start(bf16[16,5,2048]{2,1,0:T(8,128)(2,1)} %reshape.227), calls=%async_computation.3 | async-start | bytes 1048576 | tf_op jit(solution)/shard_map/while/body/eval_jaxpr/all_to_all | solution.py:163
  533.9 69.5 %reduce-scatter.4.cloned.1.call-start = ((), (), s32[]{:S(2)}) async-start(), calls=%async_computation.7 | async-start | bytes 3276800 | tf_op jit(solution)/shard_map/reduce_scatter | solution.py:208
  538.5 101.1 %reduce-scatter.8.cloned.1.call-start = ((), (), s32[]{:S(2)}) async-start(), calls=%async_computation.9 | async-start | bytes 3276800 | tf_op jit(solution)/shard_map/reduce_scatter | solution.py:214
  (50 other events, 267.1 us)
Sparse Core Ops, SparseCore 0:
  534.0 33.0 reduce-scatter.5
  569.6 33.7 reduce-scatter.3
  605.8 33.7 reduce-scatter.7
where the time goes:
time: 654 us; the launch traced here: 648 us
  waiting for transfers between devices  294 us (45%)
  local copies, waits for them, and re-layouts  107 us (16%)
  starting transfers between devices  98.3 us (15%)
  matrix products  83.7 us (13%)
  other arithmetic  49.5 us (8%)
  between operations  13.8 us (2%)
    all_to_all x5, waiting for transfers between devices, backward_step(): lax.all_to_all(outgoing.reshape(experts, cap_slots, model_width), 'expert...  55.2 us
    all_to_all x5, waiting for transfers between devices, backward_step(): lax.all_to_all(d_rows.reshape(experts, cap_slots, model_width), 'expert',...  53.7 us
    all_to_all x5, waiting for transfers between devices, forward_step(): lax.all_to_all(outgoing, 'expert', split_axis=0, concat_axis=0, tiled=True)  46.5 us
    all_to_all x5, waiting for transfers between devices, forward_step(): lax.all_to_all(produced, 'expert', split_axis=0, concat_axis=0, tiled=True)  46.3 us
    reduce_scatter x1, waiting for transfers between devices, shards(): lax.psum_scatter(local_down.astype(jnp.bfloat16), 'dp', scatter_dimension...  34 us
    reduce_scatter x1, waiting for transfers between devices, shards(): lax.psum_scatter(local_gate.astype(jnp.bfloat16), 'dp', scatter_dimension...  34 us
    dynamic_update_slice x15, other arithmetic, keep_entry(): lax.dynamic_update_index_in_dim(store, jnp.where(is_live, value, previous...  26.3 us
    reduce_scatter x1, waiting for transfers between devices, shards(): lax.psum_scatter(local_up.astype(jnp.bfloat16), 'dp', scatter_dimension=0...  24.2 us
  transfers between devices with their start and end apart: 33, of which 28 were waited for; matrix products, arithmetic and copies ran while one was open for 9% of the time, Pallas kernels for 0%

commit v1 on v0

v1 whole, which is shorter than its diff:
```python
import functools
import jax
import jax.numpy as jnp
from jax import lax
from jax.experimental import pallas as pl
from jax.experimental.pallas import tpu as pltpu
from jax.sharding import PartitionSpec as P

F32, BF16 = jnp.float32, jnp.bfloat16
epsilon = 1e-05
MESH = pl.DeviceIdType.MESH
GROUP = 1
LANES = 128
rows_by_rows = (((0,), (0,)), ((), ()))
cols_by_cols = (((1,), (1,)), ((), ()))


def inverse_rms(values):
    return lax.rsqrt(jnp.mean(values * values, -1, keepdims=True) + epsilon)


def matmul(a, b, dims=(((1,), (0,)), ((), ()))):
    return lax.dot_general(a, b, dims, preferred_element_type=F32)


def kernel(
    sizes,
    tokens, cotangent, ids, probs, gate_hbm, up_hbm, down_hbm,
    grad_gate, grad_up, grad_down,
    w_gate, w_up, w_down, base, select, select_t,
    out_a, out_b, out_r, in_a, in_b, in_r,
    carry_out, carry_in, rows, scaled_rows, work, pre_gate, pre_up,
    all_rows, all_scaled, all_gate, all_up, all_act, spread,
    load_sem, send_a, send_b, send_r, recv_a, recv_b, recv_r,
    send_carry, recv_carry, send_dp, recv_dp,
):
    batches, tokens_b, slots, cap, top, experts, n_dp = sizes
    width = base.shape[-1]
    pieces = width // LANES
    part = width // n_dp
    pairs = tokens_b * top
    section = lax.axis_index("section")
    me = lax.axis_index("expert")
    z = lax.axis_index("dp")

    def expert_at(p):
        return lax.rem(me + p, experts)

    def dp_at(q):
        return lax.rem(z + q, n_dp)

    loads = [
        pltpu.make_async_copy(gate_hbm, w_gate, load_sem.at[0]),
        pltpu.make_async_copy(up_hbm, w_up, load_sem.at[1]),
        pltpu.make_async_copy(down_hbm, w_down, load_sem.at[2]),
    ]

    @pl.when(section == 0)
    def _():
        pltpu.make_async_copy(tokens, base, load_sem.at[3]).start()

    @pl.when(section == 1)
    def _():
        pltpu.make_async_copy(cotangent, base, load_sem.at[3]).start()

    for load in loads:
        load.start()

    barrier = pltpu.get_barrier_semaphore()

    def greet(p, _):
        pl.semaphore_signal(barrier, inc=1, device_id={"expert": expert_at(p)}, device_id_type=MESH)
        return 0

    lax.fori_loop(1, experts, greet, 0)
    for q in range(1, n_dp):
        pl.semaphore_signal(barrier, inc=1, device_id={"dp": dp_at(q)}, device_id_type=MESH)
    pl.semaphore_signal(barrier, inc=1, device_id={"section": 1 - section}, device_id_type=MESH)

    def selectors(b, _):
        own = ids[b]
        order = lax.broadcasted_iota(jnp.int32, (pairs, 1), 0)
        micro = lax.rem(order, tokens_b) // (tokens_b // GROUP)
        order_l = lax.broadcasted_iota(jnp.int32, (pairs, pairs), 1)
        order_s = lax.broadcasted_iota(jnp.int32, (pairs, pairs), 0)
        micro_l = lax.rem(order_l, tokens_b) // (tokens_b // GROUP)
        before = jnp.where((order_l < order_s) & (micro_l == micro), 1.0, 0.0).astype(BF16)
        named = own == lax.broadcasted_iota(jnp.int32, (pairs, experts), 1)
        one_hot = jnp.where(named, 1.0, 0.0)
        earlier = matmul(before, one_hot.astype(BF16))
        rank = jnp.sum(earlier * one_hot, 1, keepdims=True)
        relative = lax.rem(own - me + experts, experts)
        target = (relative * (cap * GROUP) + micro * cap).astype(F32) + rank
        columns = lax.broadcasted_iota(jnp.int32, (pairs, slots), 1).astype(F32)
        select_t[b] = jnp.where(columns == target, 1.0, 0.0).astype(BF16)
        target_row = jnp.sum(jnp.where(order_l == order_s, target, 0.0), 0, keepdims=True)
        lines = lax.broadcasted_iota(jnp.int32, (slots, pairs), 0).astype(F32)
        select[b] = jnp.where(lines == target_row, 1.0, 0.0).astype(BF16)
        return 0

    lax.fori_loop(0, batches, selectors, 0)
    pl.semaphore_wait(barrier, experts - 1 + n_dp - 1 + 1)
    pltpu.make_async_copy(tokens, base, load_sem.at[3]).wait()

    def pack(values, out, own, b):
        for j in range(pieces):
            spread[pl.ds(j, slots, stride=pieces), :] = values[:, j * LANES:(j + 1) * LANES]
        out[b] = spread[...].reshape(slots, pieces, LANES).astype(BF16)
        own[b, 0:cap * GROUP] = out[b, 0:cap * GROUP]

    def unpack(tiles):
        spread[...] = tiles.astype(F32).reshape(slots * pieces, LANES)
        return [
            spread[pl.ds(j, slots, stride=pieces), :].astype(BF16) for j in range(pieces)
        ]

    def put(columns, ref, b):
        for j, column in enumerate(columns):
            ref[b, :, j * LANES:(j + 1) * LANES] = column

    chunk = cap * GROUP

    def exchange(out, into, send_sem, recv_sem, b, sign):
        def one(p, _):
            place = pl.ds(p * chunk, chunk)
            to = lax.rem(me + sign * p + experts, experts)
            pltpu.make_async_remote_copy(
                src_ref=out.at[b, place], dst_ref=into.at[b, place],
                send_sem=send_sem.at[b], recv_sem=recv_sem.at[b],
                device_id={"expert": to}, device_id_type=MESH,
            ).start()
            return 0

        lax.fori_loop(1, experts, one, 0)

    def exchanged(out, into, send_sem, recv_sem, b):
        others = pl.ds(chunk, slots - chunk)
        return pltpu.make_async_remote_copy(
            src_ref=out.at[b, others], dst_ref=into.at[b, others],
            send_sem=send_sem.at[b], recv_sem=recv_sem.at[b],
            device_id={"expert": expert_at(1)}, device_id_type=MESH,
        )

    def carry(b):
        return pltpu.make_async_remote_copy(
            src_ref=carry_out.at[b], dst_ref=carry_in.at[b],
            send_sem=send_carry.at[b], recv_sem=recv_carry.at[b],
            device_id={"section": 1 - section}, device_id_type=MESH,
        )

    def share(source, into, which, b, sliced):
        for q in range(1, n_dp):
            if sliced:
                lanes = pl.ds(pl.multiple_of(dp_at(q) * part, part), part)
                src = source.at[b, :, lanes]
            else:
                src = source.at[0, b]
            pltpu.make_async_remote_copy(
                src_ref=src, dst_ref=into.at[q, b],
                send_sem=send_dp.at[which], recv_sem=recv_dp.at[which],
                device_id={"dp": dp_at(q)}, device_id_type=MESH,
            ).start()

    def shared(into, which):
        others = into.at[pl.ds(1, n_dp - 1)]
        return pltpu.make_async_remote_copy(
            src_ref=others, dst_ref=others,
            send_sem=send_dp.at[which], recv_sem=recv_dp.at[which],
            device_id={"dp": dp_at(1)}, device_id_type=MESH,
        )

    mine = pl.ds(pl.multiple_of(z * part, part), part)

    def dispatch_rows(b, current):
        normed = (current * inverse_rms(current)).astype(BF16)
        chosen = select[b, :, 0:tokens_b] + select[b, :, tokens_b:pairs]
        pack(matmul(chosen, normed), out_a, in_a, b)
        exchange(out_a, in_a, send_a, recv_a, b, 1)

    def dispatch_scaled(b, upstream):
        weights = probs[b]
        scaled = jnp.concatenate(
            [(weights[k * tokens_b:(k + 1) * tokens_b] * upstream).astype(BF16) for k in range(top)], 0
        )
        pack(matmul(select[b], scaled), out_b, in_b, b)
        exchange(out_b, in_b, send_b, recv_b, b, 1)

    def take_rows(b):
        exchanged(out_a, in_a, send_a, recv_a, b).wait_recv()
        put(unpack(in_a[b]), rows, b)
        all_rows[0, b] = rows[b, :, mine]
        share(rows, all_rows, 0, b, True)

    def take_scaled(b):
        exchanged(out_b, in_b, send_b, recv_b, b).wait_recv()
        put(unpack(in_b[b]), scaled_rows, b)
        all_scaled[0, b] = scaled_rows[b, :, mine]
        share(scaled_rows, all_scaled, 1, b, True)

    def hidden(b):
        g = matmul(rows[b], w_gate[...])
        u = matmul(rows[b], w_up[...])
        pre_gate[b] = g
        pre_up[b] = u
        all_act[0, b] = (g * jax.nn.sigmoid(g) * u).astype(BF16)
        share(all_act, all_act, 2, b, False)

    def produce(b):
        pack(matmul(all_act[0, b], w_down[...]), out_r, in_r, b)
        exchange(out_r, in_r, send_r, recv_r, b, -1)

    def hidden_back(b):
        back = matmul(scaled_rows[b], w_down[...], cols_by_cols)
        g, u = pre_gate[b], pre_up[b]
        sg = jax.nn.sigmoid(g)
        all_gate[0, b] = (back * u * sg * (1.0 + g * (1.0 - sg))).astype(BF16)
        all_up[0, b] = (back * (g * sg)).astype(BF16)
        share(all_gate, all_gate, 3, b, False)
        share(all_up, all_up, 4, b, False)

    def produce_back(b):
        pack(
            matmul(all_gate[0, b], w_gate[...], cols_by_cols)
            + matmul(all_up[0, b], w_up[...], cols_by_cols),
            out_r, in_r, b,
        )
        exchange(out_r, in_r, send_r, recv_r, b, -1)

    def take_returned(b):
        exchanged(out_r, in_r, send_r, recv_r, b).wait_recv()
        for j, column in enumerate(unpack(in_r[b])):
            work[:, j * LANES:(j + 1) * LANES] = column
        return matmul(select_t[b], work[...])

    def combine(b):
        chosen = take_returned(b)
        weights = probs[b]
        total = weights[0:tokens_b] * chosen[0:tokens_b]
        for k in range(1, top):
            part_k = slice(k * tokens_b, (k + 1) * tokens_b)
            total = total + weights[part_k] * chosen[part_k]
        carry_out[b] = (base[b].astype(F32) + total).astype(BF16)
        carry(b).start()

    def combine_back(b):
        chosen = take_returned(b)
        d_normed = chosen[0:tokens_b]
        for k in range(1, top):
            d_normed = d_normed + chosen[k * tokens_b:(k + 1) * tokens_b]
        current = carry_in[b].astype(F32)
        scale = inverse_rms(current)
        back = scale * d_normed - current * (scale * scale * scale) * jnp.mean(
            d_normed * current, -1, keepdims=True
        )
        carry_out[b] = (base[b].astype(F32) + back).astype(BF16)
        carry(b).start()

    def wait_loads():
        for load in loads:
            load.wait()

    def loop(count, body):
        def step(i, _):
            body(i)
            return 0

        lax.fori_loop(0, count, step, 0)

    @pl.when(section == 0)
    def _():
        loop(batches, lambda b: dispatch_rows(b, base[b].astype(F32)))
        wait_loads()

        def forward(i):
            @pl.when(i < batches)
            def _():
                take_rows(i)
                hidden(i)
                produce(i)

            @pl.when(i >= 1)
            def _():
                combine(i - 1)

        loop(batches + 1, forward)

        def backward(i):
            @pl.when(i < batches)
            def _():
                carry(i).wait_recv()
                dispatch_scaled(i, carry_in[i].astype(F32))

            @pl.when(i >= 1)
            def _():
                take_scaled(i - 1)
                hidden_back(i - 1)

        loop(batches + 1, backward)

    @pl.when(section == 1)
    def _():
        loop(batches, lambda b: dispatch_scaled(b, base[b].astype(F32)))
        wait_loads()
        loop(batches, take_scaled)

        def both(i):
            @pl.when(i < batches)
            def _():
                carry(i).wait_recv()
                dispatch_rows(i, carry_in[i].astype(F32))

            @pl.when((i >= 1) & (i < batches + 1))
            def _():
                take_rows(i - 1)
                hidden(i - 1)
                hidden_back(i - 1)
                produce_back(i - 1)

            @pl.when(i >= 2)
            def _():
                combine_back(i - 2)

        loop(batches + 2, both)

    shared(all_rows, 0).wait_recv()
    shared(all_scaled, 1).wait_recv()
    shared(all_act, 2).wait_recv()
    shared(all_gate, 3).wait_recv()
    shared(all_up, 4).wait_recv()

    def add_up(q):
        def flat(ref):
            return ref[q].reshape(batches * slots, ref.shape[-1])

        gate_part = matmul(flat(all_rows), flat(all_gate), rows_by_rows)
        up_part = matmul(flat(all_rows), flat(all_up), rows_by_rows)
        down_part = matmul(flat(all_act), flat(all_scaled), rows_by_rows)

        @pl.when(q == 0)
        def _():
            grad_gate[...] = gate_part
            grad_up[...] = up_part
            grad_down[...] = down_part

        @pl.when(q > 0)
        def _():
            grad_gate[...] += gate_part
            grad_up[...] += up_part
            grad_down[...] += down_part

    loop(n_dp, add_up)

    def sent(b):
        exchanged(out_a, in_a, send_a, recv_a, b).wait_send()
        exchanged(out_b, in_b, send_b, recv_b, b).wait_send()
        exchanged(out_r, in_r, send_r, recv_r, b).wait_send()
        carry(b).wait_send()

    loop(batches, sent)
    shared(all_rows, 0).wait_send()
    shared(all_scaled, 1).wait_send()
    shared(all_act, 2).wait_send()
    shared(all_gate, 3).wait_send()
    shared(all_up, 4).wait_send()


def shards(tokens, routes, gate_probs, w_gate, w_up, w_down, cotangent):
    micro_count, row_count, width = tokens.shape
    top = routes.shape[-1]
    experts = lax.axis_size("expert")
    n_dp = lax.axis_size("dp")
    cap = min(row_count, row_count * top // experts + 1)
    hidden = w_gate.shape[-1]
    batches = micro_count // GROUP
    tokens_b = row_count * GROUP
    slots = experts * cap * GROUP
    pieces = width // LANES
    part = width // n_dp

    def columns(array):
        return array[0].reshape(batches, tokens_b, top).transpose(0, 2, 1).reshape(batches, tokens_b * top, 1)

    any_ = pl.BlockSpec(memory_space=pl.ANY)
    vmem = pl.BlockSpec(memory_space=pltpu.VMEM)
    dma = pltpu.SemaphoreType.DMA
    outs = pl.pallas_call(
        functools.partial(kernel, (batches, tokens_b, slots, cap, top, experts, n_dp)),
        out_shape=[
            jax.ShapeDtypeStruct((part, hidden), F32),
            jax.ShapeDtypeStruct((part, hidden), F32),
            jax.ShapeDtypeStruct((hidden, part), F32),
        ],
        in_specs=[any_, any_, vmem, vmem, any_, any_, any_],
        out_specs=[vmem] * 3,
        scratch_shapes=[
            pltpu.VMEM((width, hidden), BF16),
            pltpu.VMEM((width, hidden), BF16),
            pltpu.VMEM((hidden, width), BF16),
            pltpu.VMEM((batches, tokens_b, width), BF16),
            pltpu.VMEM((batches, slots, tokens_b * top), BF16),
            pltpu.VMEM((batches, tokens_b * top, slots), BF16),
            *[pltpu.VMEM((batches, slots, pieces, LANES), BF16)] * 6,
            *[pltpu.VMEM((batches, tokens_b, width), BF16)] * 2,
            *[pltpu.VMEM((batches, slots, width), BF16)] * 2,
            pltpu.VMEM((slots, width), BF16),
            *[pltpu.VMEM((batches, slots, hidden), F32)] * 2,
            *[pltpu.VMEM((n_dp, batches, slots, part), BF16)] * 2,
            *[pltpu.VMEM((n_dp, batches, slots, hidden), BF16)] * 3,
            pltpu.VMEM((slots * pieces, LANES), F32),
            dma((4,)),
            *[dma((batches,))] * 6,
            *[dma((batches,))] * 2,
            *[dma((5,))] * 2,
        ],
        compiler_params=pltpu.CompilerParams(
            collective_id=0, has_side_effects=True, vmem_limit_bytes=60 * 1024 * 1024
        ),
    )(
        tokens, cotangent, columns(routes), columns(gate_probs),
        w_gate[0, 0], w_up[0, 0], w_down[0, 0],
    )
    return tuple(out[None, None] for out in outs)


def solution(mesh):
    in_specs = (
        P(None, ("expert", "dp"), None),
        P("section", None, ("expert", "dp"), None),
        P("section", None, ("expert", "dp"), None),
        P("section", "expert", None, None),
        P("section", "expert", None, None),
        P("section", "expert", None, None),
        P(None, ("expert", "dp"), None),
    )
    out_specs = (
        P("section", "expert", "dp", None),
        P("section", "expert", "dp", None),
        P("section", "expert", None, "dp"),
    )
    return jax.shard_map(shards, mesh=mesh, in_specs=in_specs, out_specs=out_specs, check_vma=False)
```

time: 654 us -> 117 us (0.18)
  waiting for transfers between devices: 294 us -> 0 us
  Pallas kernels: 0 us -> 108 us
  local copies, waits for them, and re-layouts: 107 us -> 8.37 us
  starting transfers between devices: 98.3 us -> 0 us
  matrix products: 83.7 us -> 0 us
  other arithmetic: 49.5 us -> 0 us
  between operations: 13.8 us -> 0.65 us
    all_to_all x20 -> x0, waiting for transfers between devices: 202 us -> none  [the longest x5 55.2 us: backward_step(): lax.all_to_all(outgoing.reshape(experts, cap_slots, model_width), 'expert...]
    pallas_call x0 -> x1, Pallas kernels: none -> 108 us  [shards(): pl.pallas_call(functools.partial(kernel, (batches, tokens_b, slots, cap,...]
    reduce_scatter x3 -> x0, waiting for transfers between devices: 92.2 us -> none  [the longest x1 34 us: shards(): lax.psum_scatter(local_down.astype(jnp.bfloat16), 'dp', scatter_dimension...]
    dot_general x58 -> x0, matrix products: 83.7 us -> none  [the longest x5 17.9 us: local_backward(): lax.dot_general(arrived, weight_down, contract_cols, preferred_element_ty...]
    all_to_all x20 -> x0, starting transfers between devices: 81.8 us -> none  [the longest x5 21.4 us: forward_step(): lax.all_to_all(outgoing, 'expert', split_axis=0, concat_axis=0, tiled=True)]
    reshape x50 -> x2, local copies, waits for them, and re-layouts: 57.7 us -> 2.96 us  [columns(): array[0].reshape(batches, tokens_b, top).transpose(0, 2, 1)]
    dynamic_update_slice x15 -> x0, other arithmetic: 26.3 us -> none  [keep_entry(): lax.dynamic_update_index_in_dim(store, jnp.where(is_live, value, previous...]
    dynamic_slice x35 -> x0, local copies, waits for them, and re-layouts: 22.8 us -> none  [the longest x15 21.8 us: keep_entry(): previous = lax.dynamic_index_in_dim(store, position, 0, keepdims=False)]
  transfers between devices with their start and end apart: 33 -> 0, of which waited for: 28 -> 0; matrix products, arithmetic and copies ran while one was open for 9% -> 0% of each run, Pallas kernels for 0% -> 0%
where the time goes in v1:
time: 117 us
  Pallas kernels  108 us (92%)
  local copies, waits for them, and re-layouts  8.37 us (7%)
    pallas_call x1, Pallas kernels, shards(): pl.pallas_call(functools.partial(kernel, (batches, tokens_b, slots, cap,...  108 us
    unnamed x7, local copies, waits for them, and re-layouts  5.41 us
    reshape x2, local copies, waits for them, and re-layouts, columns(): array[0].reshape(batches, tokens_b, top).transpose(0, 2, 1)  2.96 us

profile of v1, /device:TPU:0, one launch (start us, length us, event | category | flops | bytes accessed | tf_op | source)
XLA Modules:
  0.0 117.2 jit_solution(5942425640454439728)
XLA Ops:
  0.6 1.5 %reshape.14.ids = s32[4,64,1]{2,1,0:T(8,128)} reshape(s32[4,2,32]{2,1,0:T(2,128)} %bitcast.18) | data formatting | bytes 2048 | tf_op jit(solution)/shard_map/reshape | solution.py:381
  2.1 1.5 %reshape.15.probs = f32[4,64,1]{2,1,0:T(8,128)} reshape(f32[4,2,32]{2,1,0:T(2,128)} %bitcast.19) | data formatting | bytes 2048 | tf_op jit(solution)/shard_map/reshape | solution.py:381
  3.6 108.2 %shard_map.94 = (f32[512,640]{1,0:T(8,128)}, f32[512,640]{1,0:T(8,128)}, f32[640,512]{1,0:T(8,128)}) custom-call(bf16[4,32,2048]{2,1,0:T(8,128)(2,1)} %tokens.1, bf16[4,32,2048]{2,1,0:T(8,128)(2,1)} %cotangent.1, s32[4,64,1]{2,1,0:T(8,128)} %reshape.14.ids, f32[4,64,1]{2,1,0:T(8,128)} %reshape.15.probs, bf16[2048,640]{1,0:T(8,128)(2,1)} %bitcast.12, ...), custom_call_target="tpu_custom_call" | custom-call | tf_op jit(solution)/shard_map/pallas_call | solution.py:386
  111.8 0.0 copy-start.1
  111.8 2.6 %copy.15 = f32[1,1,512,640]{3,2,1,0:T(8,128)} copy(f32[1,1,512,640]{3,2,1,0:T(8,128)} %bitcast.17) | data formatting | bytes 2621440
  114.4 0.0 copy-done.1
  114.4 0.0 copy-start
  114.4 1.1 copy.16
  115.4 0.7 copy-done
  116.2 1.1 copy.17
Async XLA Ops:
  111.8 2.6 %copy-start.1 = (f32[512,640]{1,0:T(8,128)S(1)}, f32[512,640]{1,0:T(8,128)}, u32[]{:S(2)}) copy-start(f32[512,640]{1,0:T(8,128)} %get-tuple-element.7) | copy-start | bytes 3932164
  114.4 1.8 %copy-start = (f32[640,512]{1,0:T(8,128)S(1)}, f32[640,512]{1,0:T(8,128)}, u32[]{:S(2)}) copy-start(f32[640,512]{1,0:T(8,128)} %get-tuple-element.8) | copy-start | bytes 3932164

commit v2 on v1

--- a/solution.py
+++ b/solution.py
@@ -9,7 +9,6 @@
 F32, BF16 = jnp.float32, jnp.bfloat16
 epsilon = 1e-05
 MESH = pl.DeviceIdType.MESH
-GROUP = 1
 LANES = 128
 rows_by_rows = (((0,), (0,)), ((), ()))
 cols_by_cols = (((1,), (1,)), ((), ()))
@@ -27,7 +26,7 @@
     sizes,
     tokens, cotangent, ids, probs, gate_hbm, up_hbm, down_hbm,
     grad_gate, grad_up, grad_down,
-    w_gate, w_up, w_down, base, select, select_t,
+    w_gate, w_up, w_down, base, select, select_t, weights,
     out_a, out_b, out_r, in_a, in_b, in_r,
     carry_out, carry_in, rows, scaled_rows, work, pre_gate, pre_up,
     all_rows, all_scaled, all_gate, all_up, all_act, spread,
@@ -77,20 +76,28 @@
         pl.semaphore_signal(barrier, inc=1, device_id={"dp": dp_at(q)}, device_id_type=MESH)
     pl.semaphore_signal(barrier, inc=1, device_id={"section": 1 - section}, device_id_type=MESH)
 
+    def upright(row):
+        size = row.shape[-1]
+        along = lax.broadcasted_iota(jnp.int32, (size, size), 1)
+        down = lax.broadcasted_iota(jnp.int32, (size, size), 0)
+        return jnp.sum(jnp.where(along == down, row, 0.0), 1, keepdims=True)
+
     def selectors(b, _):
-        own = ids[b]
-        order = lax.broadcasted_iota(jnp.int32, (pairs, 1), 0)
-        micro = lax.rem(order, tokens_b) // (tokens_b // GROUP)
+        named_row = ids[b].astype(F32)
+        prob_row = probs[b]
+        own = jnp.concatenate([upright(named_row[k:k + 1]) for k in range(top)], 0)
+        weights[b] = jnp.concatenate([upright(prob_row[k:k + 1]) for k in range(top)], 0)
+        own = own.astype(jnp.int32)
         order_l = lax.broadcasted_iota(jnp.int32, (pairs, pairs), 1)
         order_s = lax.broadcasted_iota(jnp.int32, (pairs, pairs), 0)
-        micro_l = lax.rem(order_l, tokens_b) // (tokens_b // GROUP)
-        before = jnp.where((order_l < order_s) & (micro_l == micro), 1.0, 0.0).astype(BF16)
+        before = jnp.where(order_l < order_s, 1.0, 0.0).astype(BF16)
         named = own == lax.broadcasted_iota(jnp.int32, (pairs, experts), 1)
         one_hot = jnp.where(named, 1.0, 0.0)
         earlier = matmul(before, one_hot.astype(BF16))
         rank = jnp.sum(earlier * one_hot, 1, keepdims=True)
-        relative = lax.rem(own - me + experts, experts)
-        target = (relative * (cap * GROUP) + micro * cap).astype(F32) + rank
+        relative = own - me
+        relative = jnp.where(relative < 0, relative + experts, relative)
+        target = (relative * cap).astype(F32) + rank
         columns = lax.broadcasted_iota(jnp.int32, (pairs, slots), 1).astype(F32)
         select_t[b] = jnp.where(columns == target, 1.0, 0.0).astype(BF16)
         target_row = jnp.sum(jnp.where(order_l == order_s, target, 0.0), 0, keepdims=True)
@@ -106,7 +113,7 @@
         for j in range(pieces):
             spread[pl.ds(j, slots, stride=pieces), :] = values[:, j * LANES:(j + 1) * LANES]
         out[b] = spread[...].reshape(slots, pieces, LANES).astype(BF16)
-        own[b, 0:cap * GROUP] = out[b, 0:cap * GROUP]
+        own[b, 0:cap] = out[b, 0:cap]
 
     def unpack(tiles):
         spread[...] = tiles.astype(F32).reshape(slots * pieces, LANES)
@@ -118,7 +125,7 @@
         for j, column in enumerate(columns):
             ref[b, :, j * LANES:(j + 1) * LANES] = column
 
-    chunk = cap * GROUP
+    chunk = cap
 
     def exchange(out, into, send_sem, recv_sem, b, sign):
         def one(p, _):
@@ -148,26 +155,36 @@
             device_id={"section": 1 - section}, device_id_type=MESH,
         )
 
-    def share(source, into, which, b, sliced):
+    def to_dp(src, into, which, b, q, to):
+        return pltpu.make_async_remote_copy(
+            src_ref=src, dst_ref=into.at[b, q],
+            send_sem=send_dp.at[which], recv_sem=recv_dp.at[which, q, b],
+            device_id={"dp": to}, device_id_type=MESH,
+        )
+
+    def share_part(source, into, which, b):
         for q in range(1, n_dp):
-            if sliced:
-                lanes = pl.ds(pl.multiple_of(dp_at(q) * part, part), part)
-                src = source.at[b, :, lanes]
-            else:
-                src = source.at[0, b]
-            pltpu.make_async_remote_copy(
-                src_ref=src, dst_ref=into.at[q, b],
-                send_sem=send_dp.at[which], recv_sem=recv_dp.at[which],
-                device_id={"dp": dp_at(q)}, device_id_type=MESH,
-            ).start()
-
-    def shared(into, which):
-        others = into.at[pl.ds(1, n_dp - 1)]
-        return pltpu.make_async_remote_copy(
+            lanes = pl.ds(pl.multiple_of(dp_at(q) * part, part), part)
+            to_dp(source.at[b, :, lanes], into, which, b, q, dp_at(q)).start()
+
+    def share(into, which, b):
+        for q in (1, n_dp - 1):
+            to_dp(into.at[b, 0], into, which, b, q, dp_at(q)).start()
+
+    def arrived(into, which, b, q):
+        to_dp(into.at[b, q], into, which, b, q, dp_at(1)).wait_recv()
+
+    def forward(into, which, b, q):
+        arrived(into, which, b, q)
+        to_dp(into.at[b, q], into, which, b, 2, dp_at(q)).start()
+
+    def left(into, which):
+        others = into.at[:, pl.ds(1, n_dp - 1)]
+        pltpu.make_async_remote_copy(
             src_ref=others, dst_ref=others,
-            send_sem=send_dp.at[which], recv_sem=recv_dp.at[which],
+            send_sem=send_dp.at[which], recv_sem=recv_dp.at[which, 0, 0],
             device_id={"dp": dp_at(1)}, device_id_type=MESH,
-        )
+        ).wait_send()
 
     mine = pl.ds(pl.multiple_of(z * part, part), part)
 
@@ -178,9 +195,8 @@
         exchange(out_a, in_a, send_a, recv_a, b, 1)
 
     def dispatch_scaled(b, upstream):
-        weights = probs[b]
         scaled = jnp.concatenate(
-            [(weights[k * tokens_b:(k + 1) * tokens_b] * upstream).astype(BF16) for k in range(top)], 0
+            [(weights[b, k * tokens_b:(k + 1) * tokens_b] * upstream).astype(BF16) for k in range(top)], 0
         )
         pack(matmul(select[b], scaled), out_b, in_b, b)
         exchange(out_b, in_b, send_b, recv_b, b, 1)
@@ -188,40 +204,40 @@
     def take_rows(b):
         exchanged(out_a, in_a, send_a, recv_a, b).wait_recv()
         put(unpack(in_a[b]), rows, b)
-        all_rows[0, b] = rows[b, :, mine]
-        share(rows, all_rows, 0, b, True)
+        all_rows[b, 0] = rows[b, :, mine]
+        share_part(rows, all_rows, 0, b)
 
     def take_scaled(b):
         exchanged(out_b, in_b, send_b, recv_b, b).wait_recv()
         put(unpack(in_b[b]), scaled_rows, b)
-        all_scaled[0, b] = scaled_rows[b, :, mine]
-        share(scaled_rows, all_scaled, 1, b, True)
+        all_scaled[b, 0] = scaled_rows[b, :, mine]
+        share_part(scaled_rows, all_scaled, 1, b)
 
     def hidden(b):
         g = matmul(rows[b], w_gate[...])
         u = matmul(rows[b], w_up[...])
         pre_gate[b] = g
         pre_up[b] = u
-        all_act[0, b] = (g * jax.nn.sigmoid(g) * u).astype(BF16)
-        share(all_act, all_act, 2, b, False)
+        all_act[b, 0] = (g * jax.nn.sigmoid(g) * u).astype(BF16)
+        share(all_act, 2, b)
 
     def produce(b):
-        pack(matmul(all_act[0, b], w_down[...]), out_r, in_r, b)
+        pack(matmul(all_act[b, 0], w_down[...]), out_r, in_r, b)
         exchange(out_r, in_r, send_r, recv_r, b, -1)
 
     def hidden_back(b):
         back = matmul(scaled_rows[b], w_down[...], cols_by_cols)
         g, u = pre_gate[b], pre_up[b]
         sg = jax.nn.sigmoid(g)
-        all_gate[0, b] = (back * u * sg * (1.0 + g * (1.0 - sg))).astype(BF16)
-        all_up[0, b] = (back * (g * sg)).astype(BF16)
-        share(all_gate, all_gate, 3, b, False)
-        share(all_up, all_up, 4, b, False)
+        all_gate[b, 0] = (back * u * sg * (1.0 + g * (1.0 - sg))).astype(BF16)
+        all_up[b, 0] = (back * (g * sg)).astype(BF16)
+        share(all_gate, 3, b)
+        share(all_up, 4, b)
 
     def produce_back(b):
         pack(
-            matmul(all_gate[0, b], w_gate[...], cols_by_cols)
-            + matmul(all_up[0, b], w_up[...], cols_by_cols),
+            matmul(all_gate[b, 0], w_gate[...], cols_by_cols)
+            + matmul(all_up[b, 0], w_up[...], cols_by_cols),
             out_r, in_r, b,
         )
         exchange(out_r, in_r, send_r, recv_r, b, -1)
@@ -234,11 +250,10 @@
 
     def combine(b):
         chosen = take_returned(b)
-        weights = probs[b]
-        total = weights[0:tokens_b] * chosen[0:tokens_b]
+        total = weights[b, 0:tokens_b] * chosen[0:tokens_b]
         for k in range(1, top):
             part_k = slice(k * tokens_b, (k + 1) * tokens_b)
-            total = total + weights[part_k] * chosen[part_k]
+            total = total + weights[b, part_k] * chosen[part_k]
         carry_out[b] = (base[b].astype(F32) + total).astype(BF16)
         carry(b).start()
 
@@ -255,6 +270,37 @@
         carry_out[b] = (base[b].astype(F32) + back).astype(BF16)
         carry(b).start()
 
+    def forward_act(b):
+        @pl.when(lax.rem(b, 2) == 0)
+        def _():
+            forward(all_act, 2, b, 1)
+
+        @pl.when(lax.rem(b, 2) == 1)
+        def _():
+            forward(all_act, 2, b, n_dp - 1)
+
+    def forward_back(b):
+        forward(all_gate, 3, b, 1)
+        forward(all_up, 4, b, n_dp - 1)
+
+    def all_arrived(b):
+        for q in range(1, n_dp):
+            arrived(all_rows, 0, b, q)
+            arrived(all_scaled, 1, b, q)
+
+        @pl.when(lax.rem(b, 2) == 0)
+        def _():
+            arrived(all_act, 2, b, n_dp - 1)
+
+        @pl.when(lax.rem(b, 2) == 1)
+        def _():
+            arrived(all_act, 2, b, 1)
+
+        arrived(all_gate, 3, b, n_dp - 1)
+        arrived(all_up, 4, b, 1)
+        for which, into in ((2, all_act), (3, all_gate), (4, all_up)):
+            arrived(into, which, b, 2)
+
     def wait_loads():
         for load in loads:
             load.wait()
@@ -289,6 +335,7 @@
             def _():
                 carry(i).wait_recv()
                 dispatch_scaled(i, carry_in[i].astype(F32))
+                forward_act(i)
 
             @pl.when(i >= 1)
             def _():
@@ -321,34 +368,33 @@
                 combine_back(i - 2)
 
         loop(batches + 2, both)
-
-    shared(all_rows, 0).wait_recv()
-    shared(all_scaled, 1).wait_recv()
-    shared(all_act, 2).wait_recv()
-    shared(all_gate, 3).wait_recv()
-    shared(all_up, 4).wait_recv()
-
-    def add_up(q):
+        loop(batches, forward_act)
+
+    loop(batches, forward_back)
+
+    def add_up(b):
+        all_arrived(b)
+
         def flat(ref):
-            return ref[q].reshape(batches * slots, ref.shape[-1])
+            return ref[b].reshape(n_dp * slots, ref.shape[-1])
 
         gate_part = matmul(flat(all_rows), flat(all_gate), rows_by_rows)
         up_part = matmul(flat(all_rows), flat(all_up), rows_by_rows)
         down_part = matmul(flat(all_act), flat(all_scaled), rows_by_rows)
 
-        @pl.when(q == 0)
+        @pl.when(b == 0)
         def _():
             grad_gate[...] = gate_part
             grad_up[...] = up_part
             grad_down[...] = down_part
 
-        @pl.when(q > 0)
+        @pl.when(b > 0)
         def _():
             grad_gate[...] += gate_part
             grad_up[...] += up_part
             grad_down[...] += down_part
 
-    loop(n_dp, add_up)
+    loop(batches, add_up)
 
     def sent(b):
         exchanged(out_a, in_a, send_a, recv_a, b).wait_send()
@@ -357,11 +403,11 @@
         carry(b).wait_send()
 
     loop(batches, sent)
-    shared(all_rows, 0).wait_send()
-    shared(all_scaled, 1).wait_send()
-    shared(all_act, 2).wait_send()
-    shared(all_gate, 3).wait_send()
-    shared(all_up, 4).wait_send()
+    left(all_rows, 0)
+    left(all_scaled, 1)
+    left(all_act, 2)
+    left(all_gate, 3)
+    left(all_up, 4)
 
 
 def shards(tokens, routes, gate_probs, w_gate, w_up, w_down, cotangent):
@@ -371,14 +417,13 @@
     n_dp = lax.axis_size("dp")
     cap = min(row_count, row_count * top // experts + 1)
     hidden = w_gate.shape[-1]
-    batches = micro_count // GROUP
-    tokens_b = row_count * GROUP
-    slots = experts * cap * GROUP
+    batches, tokens_b = micro_count, row_count
+    slots = experts * cap
     pieces = width // LANES
     part = width // n_dp
 
-    def columns(array):
-        return array[0].reshape(batches, tokens_b, top).transpose(0, 2, 1).reshape(batches, tokens_b * top, 1)
+    def in_hbm(array):
+        return pltpu.with_memory_space_constraint(array, pltpu.HBM)
 
     any_ = pl.BlockSpec(memory_space=pl.ANY)
     vmem = pl.BlockSpec(memory_space=pltpu.VMEM)
@@ -399,25 +444,27 @@
             pltpu.VMEM((batches, tokens_b, width), BF16),
             pltpu.VMEM((batches, slots, tokens_b * top), BF16),
             pltpu.VMEM((batches, tokens_b * top, slots), BF16),
+            pltpu.VMEM((batches, tokens_b * top, 1), F32),
             *[pltpu.VMEM((batches, slots, pieces, LANES), BF16)] * 6,
             *[pltpu.VMEM((batches, tokens_b, width), BF16)] * 2,
             *[pltpu.VMEM((batches, slots, width), BF16)] * 2,
             pltpu.VMEM((slots, width), BF16),
             *[pltpu.VMEM((batches, slots, hidden), F32)] * 2,
-            *[pltpu.VMEM((n_dp, batches, slots, part), BF16)] * 2,
-            *[pltpu.VMEM((n_dp, batches, slots, hidden), BF16)] * 3,
+            *[pltpu.VMEM((batches, n_dp, slots, part), BF16)] * 2,
+            *[pltpu.VMEM((batches, n_dp, slots, hidden), BF16)] * 3,
             pltpu.VMEM((slots * pieces, LANES), F32),
             dma((4,)),
             *[dma((batches,))] * 6,
             *[dma((batches,))] * 2,
-            *[dma((5,))] * 2,
+            dma((5,)),
+            dma((5, n_dp, batches)),
         ],
         compiler_params=pltpu.CompilerParams(
-            collective_id=0, has_side_effects=True, vmem_limit_bytes=60 * 1024 * 1024
+            collective_id=0, has_side_effects=True, vmem_limit_bytes=38 * 1024 * 1024
         ),
     )(
-        tokens, cotangent, columns(routes), columns(gate_probs),
-        w_gate[0, 0], w_up[0, 0], w_down[0, 0],
+        in_hbm(tokens), in_hbm(cotangent), routes[0].transpose(0, 2, 1), gate_probs[0].transpose(0, 2, 1),
+        in_hbm(w_gate[0, 0]), in_hbm(w_up[0, 0]), in_hbm(w_down[0, 0]),
     )
     return tuple(out[None, None] for out in outs)
 

time: 117 us -> 98.6 us (0.84)
  Pallas kernels: 108 us -> 93.2 us
  local copies, waits for them, and re-layouts: 8.37 us -> 4.54 us
    pallas_call x1, Pallas kernels: 108 us -> 93.2 us  [shards(): pl.pallas_call(functools.partial(kernel, (batches, tokens_b, slots, cap,...]
    reshape x2 -> x0, local copies, waits for them, and re-layouts: 2.96 us -> none  [columns(): array[0].reshape(batches, tokens_b, top).transpose(0, 2, 1)]
where the time goes in v2:
time: 98.6 us; the launch traced here: 98.4 us
  Pallas kernels  93.2 us (95%)
  local copies, waits for them, and re-layouts  4.54 us (5%)
    pallas_call x1, Pallas kernels, shards(): pl.pallas_call(functools.partial(kernel, (batches, tokens_b, slots, cap,...  93.2 us
    unnamed x7, local copies, waits for them, and re-layouts  4.54 us

profile of v2, /device:TPU:0, one launch (start us, length us, event | category | flops | bytes accessed | tf_op | source)
XLA Modules:
  0.0 98.4 jit_solution(15295884844557790643)
XLA Ops:
  0.6 0.0 copy-start
  0.6 0.7 copy-done
  1.3 0.0 copy-start.1
  1.3 0.7 copy-done.1
  2.0 93.2 %shard_map.94 = (f32[512,640]{1,0:T(8,128)S(1)}, f32[512,640]{1,0:T(8,128)S(1)}, f32[640,512]{1,0:T(8,128)S(1)}) custom-call(bf16[4,32,2048]{2,1,0:T(8,128)(2,1)} %tokens.1, bf16[4,32,2048]{2,1,0:T(8,128)(2,1)} %cotangent.1, s32[4,2,32]{2,1,0:T(2,128)S(1)} %bitcast.15, f32[4,2,32]{2,1,0:T(2,128)S(1)} %bitcast.16, bf16[2048,640]{1,0:T(8,128)(2,1)} %bitcast.17, ...), custom_call_target="tpu_custom_call" | custom-call | tf_op jit(solution)/shard_map/pallas_call | solution.py:431
  95.2 1.1 %copy.13 = f32[1,1,512,640]{3,2,1,0:T(8,128)} copy(f32[1,1,512,640]{3,2,1,0:T(8,128)S(1)} %bitcast.14) | data formatting | bytes 2621440
  96.3 1.1 %copy.14 = f32[1,1,512,640]{3,2,1,0:T(8,128)} copy(f32[1,1,512,640]{3,2,1,0:T(8,128)S(1)} %bitcast.13) | data formatting | bytes 2621440
  97.4 1.1 %copy.15 = f32[1,1,640,512]{3,2,1,0:T(8,128)} copy(f32[1,1,640,512]{3,2,1,0:T(8,128)S(1)} %bitcast.12) | data formatting | bytes 2621440
Async XLA Ops:
  0.6 0.7 copy-start
  1.3 0.7 copy-start.1

commit v3 on v2

--- a/solution.py
+++ b/solution.py
@@ -24,17 +24,18 @@
 
 def kernel(
     sizes,
-    tokens, cotangent, ids, probs, gate_hbm, up_hbm, down_hbm,
+    tokens, cotangent, ids_hbm, probs_hbm, gate_hbm, up_hbm, down_hbm,
     grad_gate, grad_up, grad_down,
-    w_gate, w_up, w_down, base, select, select_t, weights,
+    ids, probs, w_hidden, w_down, w_hidden_t, w_down_t, base, select, select_t, weights,
     out_a, out_b, out_r, in_a, in_b, in_r,
-    carry_out, carry_in, rows, scaled_rows, work, pre_gate, pre_up,
-    all_rows, all_scaled, all_gate, all_up, all_act, spread,
+    carry_out, carry_in, rows, scaled_rows, work, pre_hidden,
+    all_rows, all_scaled, all_back, all_act, spread,
     load_sem, send_a, send_b, send_r, recv_a, recv_b, recv_r,
     send_carry, recv_carry, send_dp, recv_dp,
 ):
     batches, tokens_b, slots, cap, top, experts, n_dp = sizes
     width = base.shape[-1]
+    units = w_down.shape[0]
     pieces = width // LANES
     part = width // n_dp
     pairs = tokens_b * top
@@ -49,8 +50,8 @@
         return lax.rem(z + q, n_dp)
 
     loads = [
-        pltpu.make_async_copy(gate_hbm, w_gate, load_sem.at[0]),
-        pltpu.make_async_copy(up_hbm, w_up, load_sem.at[1]),
+        pltpu.make_async_copy(gate_hbm, w_hidden.at[:, pl.ds(0, units)], load_sem.at[0]),
+        pltpu.make_async_copy(up_hbm, w_hidden.at[:, pl.ds(units, units)], load_sem.at[1]),
         pltpu.make_async_copy(down_hbm, w_down, load_sem.at[2]),
     ]
 
@@ -62,7 +63,11 @@
     def _():
         pltpu.make_async_copy(cotangent, base, load_sem.at[3]).start()
 
-    for load in loads:
+    tables = [
+        pltpu.make_async_copy(ids_hbm, ids, load_sem.at[4]),
+        pltpu.make_async_copy(probs_hbm, probs, load_sem.at[5]),
+    ]
+    for load in tables + loads:
         load.start()
 
     barrier = pltpu.get_barrier_semaphore()
@@ -82,7 +87,7 @@
         down = lax.broadcasted_iota(jnp.int32, (size, size), 0)
         return jnp.sum(jnp.where(along == down, row, 0.0), 1, keepdims=True)
 
-    def selectors(b, _):
+    def selectors(b):
         named_row = ids[b].astype(F32)
         prob_row = probs[b]
         own = jnp.concatenate([upright(named_row[k:k + 1]) for k in range(top)], 0)
@@ -103,10 +108,9 @@
         target_row = jnp.sum(jnp.where(order_l == order_s, target, 0.0), 0, keepdims=True)
         lines = lax.broadcasted_iota(jnp.int32, (slots, pairs), 0).astype(F32)
         select[b] = jnp.where(lines == target_row, 1.0, 0.0).astype(BF16)
-        return 0
-
-    lax.fori_loop(0, batches, selectors, 0)
-    pl.semaphore_wait(barrier, experts - 1 + n_dp - 1 + 1)
+
+    for load in tables:
+        load.wait()
     pltpu.make_async_copy(tokens, base, load_sem.at[3]).wait()
 
     def pack(values, out, own, b):
@@ -188,17 +192,29 @@
 
     mine = pl.ds(pl.multiple_of(z * part, part), part)
 
-    def dispatch_rows(b, current):
+    def pack_rows(b, current):
         normed = (current * inverse_rms(current)).astype(BF16)
         chosen = select[b, :, 0:tokens_b] + select[b, :, tokens_b:pairs]
         pack(matmul(chosen, normed), out_a, in_a, b)
+
+    def dispatch_rows(b, current):
+        pack_rows(b, current)
+        send_rows(b)
+
+    def send_rows(b):
         exchange(out_a, in_a, send_a, recv_a, b, 1)
 
-    def dispatch_scaled(b, upstream):
+    def pack_scaled(b, upstream):
         scaled = jnp.concatenate(
             [(weights[b, k * tokens_b:(k + 1) * tokens_b] * upstream).astype(BF16) for k in range(top)], 0
         )
         pack(matmul(select[b], scaled), out_b, in_b, b)
+
+    def dispatch_scaled(b, upstream):
+        pack_scaled(b, upstream)
+        send_scaled(b)
+
+    def send_scaled(b):
         exchange(out_b, in_b, send_b, recv_b, b, 1)
 
     def take_rows(b):
@@ -214,10 +230,9 @@
         share_part(scaled_rows, all_scaled, 1, b)
 
     def hidden(b):
-        g = matmul(rows[b], w_gate[...])
-        u = matmul(rows[b], w_up[...])
-        pre_gate[b] = g
-        pre_up[b] = u
+        pre = matmul(rows[b], w_hidden[...])
+        pre_hidden[b] = pre
+        g, u = pre[:, 0:units], pre[:, units:2 * units]
         all_act[b, 0] = (g * jax.nn.sigmoid(g) * u).astype(BF16)
         share(all_act, 2, b)
 
@@ -226,21 +241,24 @@
         exchange(out_r, in_r, send_r, recv_r, b, -1)
 
     def hidden_back(b):
-        back = matmul(scaled_rows[b], w_down[...], cols_by_cols)
-        g, u = pre_gate[b], pre_up[b]
+        back = matmul(scaled_rows[b], w_down_t[...])
+        g, u = pre_hidden[b, :, 0:units], pre_hidden[b, :, units:2 * units]
         sg = jax.nn.sigmoid(g)
-        all_gate[b, 0] = (back * u * sg * (1.0 + g * (1.0 - sg))).astype(BF16)
-        all_up[b, 0] = (back * (g * sg)).astype(BF16)
-        share(all_gate, 3, b)
-        share(all_up, 4, b)
+        all_back[b, 0, :, 0:units] = (back * u * sg * (1.0 + g * (1.0 - sg))).astype(BF16)
+        all_back[b, 0, :, units:2 * units] = (back * (g * sg)).astype(BF16)
+        share(all_back, 3, b)
 
     def produce_back(b):
-        pack(
-            matmul(all_gate[b, 0], w_gate[...], cols_by_cols)
-            + matmul(all_up[b, 0], w_up[...], cols_by_cols),
-            out_r, in_r, b,
-        )
+        pack(matmul(all_back[b, 0], w_hidden_t[...]), out_r, in_r, b)
         exchange(out_r, in_r, send_r, recv_r, b, -1)
+
+    def turn_down(b):
+        place = pl.ds(pl.multiple_of(b * (width // batches), width // batches), width // batches)
+        w_down_t[place, :] = w_down[:, place].T
+
+    def turn_hidden(b):
+        place = pl.ds(pl.multiple_of(b * (width // batches), width // batches), width // batches)
+        w_hidden_t[:, place] = w_hidden[place, :].T
 
     def take_returned(b):
         exchanged(out_r, in_r, send_r, recv_r, b).wait_recv()
@@ -280,8 +298,13 @@
             forward(all_act, 2, b, n_dp - 1)
 
     def forward_back(b):
-        forward(all_gate, 3, b, 1)
-        forward(all_up, 4, b, n_dp - 1)
+        for q, lanes in ((1, pl.ds(0, units)), (n_dp - 1, pl.ds(units, units))):
+            arrived(all_back, 3, b, q)
+            pltpu.make_async_remote_copy(
+                src_ref=all_back.at[b, q, :, lanes], dst_ref=all_back.at[b, 2, :, lanes],
+                send_sem=send_dp.at[3], recv_sem=recv_dp.at[3, 2, b],
+                device_id={"dp": dp_at(q)}, device_id_type=MESH,
+            ).start()
 
     def all_arrived(b):
         for q in range(1, n_dp):
@@ -296,28 +319,43 @@
         def _():
             arrived(all_act, 2, b, 1)
 
-        arrived(all_gate, 3, b, n_dp - 1)
-        arrived(all_up, 4, b, 1)
-        for which, into in ((2, all_act), (3, all_gate), (4, all_up)):
-            arrived(into, which, b, 2)
+        arrived(all_act, 2, b, 2)
+        arrived(all_back, 3, b, 2)
 
     def wait_loads():
         for load in loads:
             load.wait()
 
-    def loop(count, body):
+    def loop(count, body, first=0):
         def step(i, _):
             body(i)
             return 0
 
-        lax.fori_loop(0, count, step, 0)
+        lax.fori_loop(first, count, step, 0)
+
+    selectors(0)
 
     @pl.when(section == 0)
     def _():
-        loop(batches, lambda b: dispatch_rows(b, base[b].astype(F32)))
+        pack_rows(0, base[0].astype(F32))
+
+    @pl.when(section == 1)
+    def _():
+        pack_scaled(0, base[0].astype(F32))
+
+    pl.semaphore_wait(barrier, experts - 1 + n_dp - 1 + 1)
+
+    @pl.when(section == 0)
+    def _():
+        def start(b):
+            selectors(b)
+            dispatch_rows(b, base[b].astype(F32))
+
+        send_rows(0)
+        loop(batches, start, 1)
         wait_loads()
 
-        def forward(i):
+        def forward_step(i):
             @pl.when(i < batches)
             def _():
                 take_rows(i)
@@ -328,7 +366,8 @@
             def _():
                 combine(i - 1)
 
-        loop(batches + 1, forward)
+        loop(batches + 1, forward_step)
+        loop(batches, turn_down)
 
         def backward(i):
             @pl.when(i < batches)
@@ -342,13 +381,28 @@
                 take_scaled(i - 1)
                 hidden_back(i - 1)
 
+            @pl.when(i >= 2)
+            def _():
+                forward_back(i - 2)
+
         loop(batches + 1, backward)
 
     @pl.when(section == 1)
     def _():
-        loop(batches, lambda b: dispatch_scaled(b, base[b].astype(F32)))
+        def start(b):
+            selectors(b)
+            dispatch_scaled(b, base[b].astype(F32))
+
+        send_scaled(0)
+        loop(batches, start, 1)
         wait_loads()
-        loop(batches, take_scaled)
+
+        def prepare(b):
+            turn_down(b)
+            take_scaled(b)
+            turn_hidden(b)
+
+        loop(batches, prepare)
 
         def both(i):
             @pl.when(i < batches)
@@ -366,11 +420,10 @@
             @pl.when(i >= 2)
             def _():
                 combine_back(i - 2)
+                forward_act(i - 2)
+                forward_back(i - 2)
 
         loop(batches + 2, both)
-        loop(batches, forward_act)
-
-    loop(batches, forward_back)
 
     def add_up(b):
         all_arrived(b)
@@ -378,8 +431,8 @@
         def flat(ref):
             return ref[b].reshape(n_dp * slots, ref.shape[-1])
 
-        gate_part = matmul(flat(all_rows), flat(all_gate), rows_by_rows)
-        up_part = matmul(flat(all_rows), flat(all_up), rows_by_rows)
+        both = matmul(flat(all_rows), flat(all_back), rows_by_rows)
+        gate_part, up_part = both[:, 0:units], both[:, units:2 * units]
         down_part = matmul(flat(all_act), flat(all_scaled), rows_by_rows)
 
         @pl.when(b == 0)
@@ -394,7 +447,13 @@
             grad_up[...] += up_part
             grad_down[...] += down_part
 
-    loop(batches, add_up)
+    add_up(0)
+
+    @pl.when(section == 0)
+    def _():
+        forward_back(batches - 1)
+
+    loop(batches, add_up, 1)
 
     def sent(b):
         exchanged(out_a, in_a, send_a, recv_a, b).wait_send()
@@ -406,8 +465,7 @@
     left(all_rows, 0)
     left(all_scaled, 1)
     left(all_act, 2)
-    left(all_gate, 3)
-    left(all_up, 4)
+    left(all_back, 3)
 
 
 def shards(tokens, routes, gate_probs, w_gate, w_up, w_down, cotangent):
@@ -435,12 +493,15 @@
             jax.ShapeDtypeStruct((part, hidden), F32),
             jax.ShapeDtypeStruct((hidden, part), F32),
         ],
-        in_specs=[any_, any_, vmem, vmem, any_, any_, any_],
+        in_specs=[any_] * 7,
         out_specs=[vmem] * 3,
         scratch_shapes=[
+            pltpu.VMEM((batches, top, tokens_b), jnp.int32),
+            pltpu.VMEM((batches, top, tokens_b), F32),
+            pltpu.VMEM((width, 2 * hidden), BF16),
+            pltpu.VMEM((hidden, width), BF16),
+            pltpu.VMEM((2 * hidden, width), BF16),
             pltpu.VMEM((width, hidden), BF16),
-            pltpu.VMEM((width, hidden), BF16),
-            pltpu.VMEM((hidden, width), BF16),
             pltpu.VMEM((batches, tokens_b, width), BF16),
             pltpu.VMEM((batches, slots, tokens_b * top), BF16),
             pltpu.VMEM((batches, tokens_b * top, slots), BF16),
@@ -449,21 +510,23 @@
             *[pltpu.VMEM((batches, tokens_b, width), BF16)] * 2,
             *[pltpu.VMEM((batches, slots, width), BF16)] * 2,
             pltpu.VMEM((slots, width), BF16),
-            *[pltpu.VMEM((batches, slots, hidden), F32)] * 2,
+            pltpu.VMEM((batches, slots, 2 * hidden), F32),
             *[pltpu.VMEM((batches, n_dp, slots, part), BF16)] * 2,
-            *[pltpu.VMEM((batches, n_dp, slots, hidden), BF16)] * 3,
+            pltpu.VMEM((batches, n_dp, slots, 2 * hidden), BF16),
+            pltpu.VMEM((batches, n_dp, slots, hidden), BF16),
             pltpu.VMEM((slots * pieces, LANES), F32),
-            dma((4,)),
+            dma((6,)),
             *[dma((batches,))] * 6,
             *[dma((batches,))] * 2,
-            dma((5,)),
-            dma((5, n_dp, batches)),
+            dma((4,)),
+            dma((4, n_dp, batches)),
         ],
         compiler_params=pltpu.CompilerParams(
-            collective_id=0, has_side_effects=True, vmem_limit_bytes=38 * 1024 * 1024
+            collective_id=0, has_side_effects=True, vmem_limit_bytes=46 * 1024 * 1024
         ),
     )(
-        in_hbm(tokens), in_hbm(cotangent), routes[0].transpose(0, 2, 1), gate_probs[0].transpose(0, 2, 1),
+        in_hbm(tokens), in_hbm(cotangent),
+        in_hbm(routes[0].transpose(0, 2, 1)), in_hbm(gate_probs[0].transpose(0, 2, 1)),
         in_hbm(w_gate[0, 0]), in_hbm(w_up[0, 0]), in_hbm(w_down[0, 0]),
     )
     return tuple(out[None, None] for out in outs)

time: 98.6 us -> 94.1 us (0.954)
  Pallas kernels: 93.2 us -> 90.1 us
  local copies, waits for them, and re-layouts: 4.54 us -> 3.17 us
    pallas_call x1, Pallas kernels: 93.2 us -> 90.1 us  [shards(): pl.pallas_call(functools.partial(kernel, (batches, tokens_b, slots, cap,...]
    unnamed x7 -> x3, local copies, waits for them, and re-layouts: 4.54 us -> 3.17 us
where the time goes in v3:
time: 94.1 us; the launch traced here: 94 us
  Pallas kernels  90.1 us (96%)
  local copies, waits for them, and re-layouts  3.17 us (3%)
    pallas_call x1, Pallas kernels, shards(): pl.pallas_call(functools.partial(kernel, (batches, tokens_b, slots, cap,...  90.1 us
    unnamed x3, local copies, waits for them, and re-layouts  3.17 us

profile of v3, /device:TPU:0, one launch (start us, length us, event | category | flops | bytes accessed | tf_op | source)
XLA Modules:
  0.0 94.0 jit_solution(1823818154249320710)
XLA Ops:
  0.6 90.1 %shard_map.94 = (f32[512,640]{1,0:T(8,128)S(1)}, f32[512,640]{1,0:T(8,128)S(1)}, f32[640,512]{1,0:T(8,128)S(1)}) custom-call(bf16[4,32,2048]{2,1,0:T(8,128)(2,1)} %tokens.1, bf16[4,32,2048]{2,1,0:T(8,128)(2,1)} %cotangent.1, s32[4,2,32]{2,1,0:T(2,128)} %bitcast.18, f32[4,2,32]{2,1,0:T(2,128)} %bitcast.19, bf16[2048,640]{1,0:T(8,128)(2,1)} %bitcast.15, ...), custom_call_target="tpu_custom_call" | custom-call | tf_op jit(solution)/shard_map/pallas_call | solution.py:489
  90.8 1.1 %copy.13 = f32[1,1,512,640]{3,2,1,0:T(8,128)} copy(f32[1,1,512,640]{3,2,1,0:T(8,128)S(1)} %bitcast.14) | data formatting | bytes 2621440
  91.8 1.1 %copy.14 = f32[1,1,512,640]{3,2,1,0:T(8,128)} copy(f32[1,1,512,640]{3,2,1,0:T(8,128)S(1)} %bitcast.13) | data formatting | bytes 2621440
  92.9 1.1 %copy.15 = f32[1,1,640,512]{3,2,1,0:T(8,128)} copy(f32[1,1,640,512]{3,2,1,0:T(8,128)S(1)} %bitcast.12) | data formatting | bytes 2621440

commit v4 on v3

--- a/solution.py
+++ b/solution.py
@@ -30,8 +30,10 @@
     out_a, out_b, out_r, in_a, in_b, in_r,
     carry_out, carry_in, rows, scaled_rows, work, pre_hidden,
     all_rows, all_scaled, all_back, all_act, spread,
+    early_out, early_in, ids_in, probs_in, tiles_out, tiles_in,
     load_sem, send_a, send_b, send_r, recv_a, recv_b, recv_r,
     send_carry, recv_carry, send_dp, recv_dp,
+    send_early, recv_early,
 ):
     batches, tokens_b, slots, cap, top, experts, n_dp = sizes
     width = base.shape[-1]
@@ -87,27 +89,35 @@
         down = lax.broadcasted_iota(jnp.int32, (size, size), 0)
         return jnp.sum(jnp.where(along == down, row, 0.0), 1, keepdims=True)
 
-    def selectors(b):
-        named_row = ids[b].astype(F32)
-        prob_row = probs[b]
-        own = jnp.concatenate([upright(named_row[k:k + 1]) for k in range(top)], 0)
-        weights[b] = jnp.concatenate([upright(prob_row[k:k + 1]) for k in range(top)], 0)
-        own = own.astype(jnp.int32)
+    def places(named_ids, by_slot=False):
+        named_row = named_ids.astype(F32)
+        own = jnp.concatenate([upright(named_row[k:k + 1]) for k in range(top)], 0).astype(jnp.int32)
         order_l = lax.broadcasted_iota(jnp.int32, (pairs, pairs), 1)
         order_s = lax.broadcasted_iota(jnp.int32, (pairs, pairs), 0)
         before = jnp.where(order_l < order_s, 1.0, 0.0).astype(BF16)
-        named = own == lax.broadcasted_iota(jnp.int32, (pairs, experts), 1)
-        one_hot = jnp.where(named, 1.0, 0.0)
+        one_hot = jnp.where(own == lax.broadcasted_iota(jnp.int32, (pairs, experts), 1), 1.0, 0.0)
         earlier = matmul(before, one_hot.astype(BF16))
         rank = jnp.sum(earlier * one_hot, 1, keepdims=True)
         relative = own - me
         relative = jnp.where(relative < 0, relative + experts, relative)
-        target = (relative * cap).astype(F32) + rank
+        relative = relative.astype(F32)
+        target = rank * experts + relative if by_slot else relative * cap + rank
+        target_row = jnp.sum(jnp.where(order_l == order_s, target, 0.0), 0, keepdims=True)
+        return target, target_row
+
+    def selector(target_row):
+        lines = lax.broadcasted_iota(jnp.int32, (slots, pairs), 0).astype(F32)
+        return jnp.where(lines == target_row, 1.0, 0.0).astype(BF16)
+
+    def weights_of(prob_row):
+        return jnp.concatenate([upright(prob_row[k:k + 1]) for k in range(top)], 0)
+
+    def selectors(b):
+        weights[b] = weights_of(probs[b])
+        target, target_row = places(ids[b])
         columns = lax.broadcasted_iota(jnp.int32, (pairs, slots), 1).astype(F32)
         select_t[b] = jnp.where(columns == target, 1.0, 0.0).astype(BF16)
-        target_row = jnp.sum(jnp.where(order_l == order_s, target, 0.0), 0, keepdims=True)
-        lines = lax.broadcasted_iota(jnp.int32, (slots, pairs), 0).astype(F32)
-        select[b] = jnp.where(lines == target_row, 1.0, 0.0).astype(BF16)
+        select[b] = selector(target_row)
 
     for load in tables:
         load.wait()
@@ -119,15 +129,10 @@
         out[b] = spread[...].reshape(slots, pieces, LANES).astype(BF16)
         own[b, 0:cap] = out[b, 0:cap]
 
-    def unpack(tiles):
+    def unpack(tiles, ref):
         spread[...] = tiles.astype(F32).reshape(slots * pieces, LANES)
-        return [
-            spread[pl.ds(j, slots, stride=pieces), :].astype(BF16) for j in range(pieces)
-        ]
-
-    def put(columns, ref, b):
-        for j, column in enumerate(columns):
-            ref[b, :, j * LANES:(j + 1) * LANES] = column
+        for j in range(pieces):
+            ref[:, j * LANES:(j + 1) * LANES] = spread[pl.ds(j, slots, stride=pieces), :].astype(BF16)
 
     chunk = cap
 
@@ -190,12 +195,90 @@
             device_id={"dp": dp_at(1)}, device_id_type=MESH,
         ).wait_send()
 
+    pieces_part = part // LANES
+    cap_all = cap * batches
+
+    def early(src, dst, which, q, to):
+        return pltpu.make_async_remote_copy(
+            src_ref=src, dst_ref=dst, send_sem=send_early.at[which], recv_sem=recv_early.at[which, q],
+            device_id={"dp": to}, device_id_type=MESH,
+        )
+
+    def early_tiles(q, p, sem, to):
+        return pltpu.make_async_remote_copy(
+            src_ref=tiles_out.at[q, p], dst_ref=tiles_in.at[q, p],
+            send_sem=send_early.at[3], recv_sem=recv_early.at[3, sem],
+            device_id={"expert": to}, device_id_type=MESH,
+        )
+
+    def early_send(source, b):
+        for q in range(1, n_dp):
+            lanes = pl.ds(pl.multiple_of(dp_at(q) * part, part), part)
+            early(source.at[b, :, lanes], early_in.at[q, b], 0, q, dp_at(q)).start()
+
+    def early_tables():
+        for q in range(1, n_dp):
+            early(ids, ids_in.at[q], 1, q, dp_at(q)).start()
+            early(probs, probs_in.at[q], 2, q, dp_at(q)).start()
+
+    def early_dispatch(q):
+        for which, into in enumerate((early_in, ids_in, probs_in)):
+            early(into.at[q], into.at[q], which, q, dp_at(1)).wait_recv()
+        for b in range(batches):
+            picked = selector(places(ids_in[q, b], True)[1])
+            weight = weights_of(probs_in[q, b])
+            values = early_in[q, b].astype(F32)
+            scaled = jnp.concatenate(
+                [
+                    (jnp.where(section == 0, 1.0, weight[k * tokens_b:(k + 1) * tokens_b]) * values).astype(BF16)
+                    for k in range(top)
+                ],
+                0,
+            )
+            out = matmul(picked, scaled)
+            for slot in range(cap):
+                for j in range(pieces_part):
+                    spread[pl.ds(j * cap_all + b * cap + slot, experts, stride=cap_all * pieces_part), :] = out[
+                        slot * experts:(slot + 1) * experts, j * LANES:(j + 1) * LANES
+                    ]
+        tiles_out[q] = spread[...].reshape(experts, cap_all * pieces_part, LANES).astype(BF16)
+        tiles_in[q, 0] = tiles_out[q, 0]
+
+        def one(p, _):
+            early_tiles(q, p, q, expert_at(p)).start()
+            return 0
+
+        lax.fori_loop(1, experts, one, 0)
+
+    def early_take(q):
+        early_tiles(q, pl.ds(1, experts - 1), q, expert_at(1)).wait_recv()
+        spread[...] = tiles_in[q].astype(F32).reshape(slots * pieces, LANES)
+        down = lax.broadcasted_iota(jnp.int32, (slots, slots), 0)
+        along = lax.broadcasted_iota(jnp.int32, (slots, slots), 1)
+        order = jnp.where(lax.rem(down, cap) * experts + down // cap == along, 1.0, 0.0).astype(BF16)
+        for b in range(batches):
+            for slot in range(cap):
+                for j in range(pieces_part):
+                    work[slot * experts:(slot + 1) * experts, j * LANES:(j + 1) * LANES] = spread[
+                        pl.ds(j * cap_all + b * cap + slot, experts, stride=cap_all * pieces_part), :
+                    ].astype(BF16)
+            block = matmul(order, work[:, 0:part]).astype(BF16)
+
+            @pl.when(section == 0)
+            def _():
+                all_rows[b, q] = block
+
+            @pl.when(section == 1)
+            def _():
+                all_scaled[b, q] = block
+
     mine = pl.ds(pl.multiple_of(z * part, part), part)
 
     def pack_rows(b, current):
         normed = (current * inverse_rms(current)).astype(BF16)
         chosen = select[b, :, 0:tokens_b] + select[b, :, tokens_b:pairs]
         pack(matmul(chosen, normed), out_a, in_a, b)
+        early_out[b] = normed
 
     def dispatch_rows(b, current):
         pack_rows(b, current)
@@ -219,15 +302,21 @@
 
     def take_rows(b):
         exchanged(out_a, in_a, send_a, recv_a, b).wait_recv()
-        put(unpack(in_a[b]), rows, b)
+        unpack(in_a[b], rows.at[b])
         all_rows[b, 0] = rows[b, :, mine]
-        share_part(rows, all_rows, 0, b)
+
+        @pl.when(section == 1)
+        def _():
+            share_part(rows, all_rows, 0, b)
 
     def take_scaled(b):
         exchanged(out_b, in_b, send_b, recv_b, b).wait_recv()
-        put(unpack(in_b[b]), scaled_rows, b)
+        unpack(in_b[b], scaled_rows.at[b])
         all_scaled[b, 0] = scaled_rows[b, :, mine]
-        share_part(scaled_rows, all_scaled, 1, b)
+
+        @pl.when(section == 0)
+        def _():
+            share_part(scaled_rows, all_scaled, 1, b)
 
     def hidden(b):
         pre = matmul(rows[b], w_hidden[...])
@@ -262,8 +351,7 @@
 
     def take_returned(b):
         exchanged(out_r, in_r, send_r, recv_r, b).wait_recv()
-        for j, column in enumerate(unpack(in_r[b])):
-            work[:, j * LANES:(j + 1) * LANES] = column
+        unpack(in_r[b], work)
         return matmul(select_t[b], work[...])
 
     def combine(b):
@@ -307,9 +395,15 @@
             ).start()
 
     def all_arrived(b):
-        for q in range(1, n_dp):
-            arrived(all_rows, 0, b, q)
-            arrived(all_scaled, 1, b, q)
+        @pl.when(section == 0)
+        def _():
+            for q in range(1, n_dp):
+                arrived(all_scaled, 1, b, q)
+
+        @pl.when(section == 1)
+        def _():
+            for q in range(1, n_dp):
+                arrived(all_rows, 0, b, q)
 
         @pl.when(lax.rem(b, 2) == 0)
         def _():
@@ -350,8 +444,11 @@
         def start(b):
             selectors(b)
             dispatch_rows(b, base[b].astype(F32))
+            early_send(early_out, b)
 
         send_rows(0)
+        early_send(early_out, 0)
+        early_tables()
         loop(batches, start, 1)
         wait_loads()
 
@@ -368,6 +465,7 @@
 
         loop(batches + 1, forward_step)
         loop(batches, turn_down)
+        loop(n_dp, early_dispatch, 1)
 
         def backward(i):
             @pl.when(i < batches)
@@ -392,17 +490,21 @@
         def start(b):
             selectors(b)
             dispatch_scaled(b, base[b].astype(F32))
+            early_send(base, b)
 
         send_scaled(0)
+        loop(batches, lambda b: early_send(base, b))
+        early_tables()
+
+        def start(b):
+            selectors(b)
+            pack_scaled(b, base[b].astype(F32))
+
         loop(batches, start, 1)
+        loop(2, send_scaled, 1)
         wait_loads()
-
-        def prepare(b):
-            turn_down(b)
-            take_scaled(b)
-            turn_hidden(b)
-
-        loop(batches, prepare)
+        loop(batches, turn_down)
+        loop(batches, turn_hidden)
 
         def both(i):
             @pl.when(i < batches)
@@ -410,10 +512,15 @@
                 carry(i).wait_recv()
                 dispatch_rows(i, carry_in[i].astype(F32))
 
+            @pl.when(i + 2 < batches)
+            def _():
+                send_scaled(i + 2)
+
             @pl.when((i >= 1) & (i < batches + 1))
             def _():
                 take_rows(i - 1)
                 hidden(i - 1)
+                take_scaled(i - 1)
                 hidden_back(i - 1)
                 produce_back(i - 1)
 
@@ -424,6 +531,7 @@
                 forward_back(i - 2)
 
         loop(batches + 2, both)
+        loop(n_dp, early_dispatch, 1)
 
     def add_up(b):
         all_arrived(b)
@@ -447,6 +555,7 @@
             grad_up[...] += up_part
             grad_down[...] += down_part
 
+    loop(n_dp, early_take, 1)
     add_up(0)
 
     @pl.when(section == 0)
@@ -462,10 +571,27 @@
         carry(b).wait_send()
 
     loop(batches, sent)
-    left(all_rows, 0)
-    left(all_scaled, 1)
+    @pl.when(section == 0)
+    def _():
+        left(all_scaled, 1)
+
+    @pl.when(section == 1)
+    def _():
+        left(all_rows, 0)
+
+    for which, into in enumerate((early_in, ids_in, probs_in)):
+        early(into.at[pl.ds(1, n_dp - 1)], into.at[pl.ds(1, n_dp - 1)], which, 0, dp_at(1)).wait_send()
+    early_tiles(pl.ds(1, n_dp - 1), pl.ds(1, experts - 1), 0, expert_at(1)).wait_send()
     left(all_act, 2)
     left(all_back, 3)
+
+
+def hand_over(*refs):
+    copies = [pltpu.make_async_copy(refs[i], refs[3 + i], refs[6].at[i]) for i in range(3)]
+    for copy in copies:
+        copy.start()
+    for copy in copies:
+        copy.wait()
 
 
 def shards(tokens, routes, gate_probs, w_gate, w_up, w_down, cotangent):
@@ -515,20 +641,35 @@
             pltpu.VMEM((batches, n_dp, slots, 2 * hidden), BF16),
             pltpu.VMEM((batches, n_dp, slots, hidden), BF16),
             pltpu.VMEM((slots * pieces, LANES), F32),
+            pltpu.VMEM((batches, tokens_b, width), BF16),
+            pltpu.VMEM((n_dp, batches, tokens_b, part), BF16),
+            pltpu.VMEM((n_dp, batches, top, tokens_b), jnp.int32),
+            pltpu.VMEM((n_dp, batches, top, tokens_b), F32),
+            *[pltpu.VMEM((n_dp, experts, cap * batches * part // LANES, LANES), BF16)] * 2,
             dma((6,)),
             *[dma((batches,))] * 6,
             *[dma((batches,))] * 2,
             dma((4,)),
             dma((4, n_dp, batches)),
+            dma((4,)),
+            dma((4, n_dp)),
         ],
         compiler_params=pltpu.CompilerParams(
-            collective_id=0, has_side_effects=True, vmem_limit_bytes=46 * 1024 * 1024
+            collective_id=0, has_side_effects=True, vmem_limit_bytes=50 * 1024 * 1024
         ),
     )(
         in_hbm(tokens), in_hbm(cotangent),
         in_hbm(routes[0].transpose(0, 2, 1)), in_hbm(gate_probs[0].transpose(0, 2, 1)),
         in_hbm(w_gate[0, 0]), in_hbm(w_up[0, 0]), in_hbm(w_down[0, 0]),
     )
+    outs = pl.pallas_call(
+        hand_over,
+        out_shape=[pltpu.HBM(out.shape, out.dtype) for out in outs],
+        in_specs=[any_] * 3,
+        out_specs=[any_] * 3,
+        scratch_shapes=[dma((3,))],
+        compiler_params=pltpu.CompilerParams(vmem_limit_bytes=4 * 1024 * 1024),
+    )(*outs)
     return tuple(out[None, None] for out in outs)
 
 

time: 94.1 us -> 91.6 us (0.973)
  local copies, waits for them, and re-layouts: 3.17 us -> 0 us
    unnamed x3 -> x0, local copies, waits for them, and re-layouts: 3.17 us -> none
    pallas_call x0 -> x1, Pallas kernels: none -> 1.95 us  [shards(): pl.pallas_call(hand_over, out_shape=[pltpu.HBM(out.shape, out.dtype) for...]
    pallas_call x1, Pallas kernels: 90.1 us -> 88.7 us  [shards(): pl.pallas_call(functools.partial(kernel, (batches, tokens_b, slots, cap,...]
where the time goes in v4:
time: 91.6 us; the launch traced here: 91.5 us
  Pallas kernels  90.7 us (99%)
    pallas_call x1, Pallas kernels, shards(): pl.pallas_call(functools.partial(kernel, (batches, tokens_b, slots, cap,...  88.7 us
    pallas_call x1, Pallas kernels, shards(): pl.pallas_call(hand_over, out_shape=[pltpu.HBM(out.shape, out.dtype) for...  1.95 us

profile of v4, /device:TPU:0, one launch (start us, length us, event | category | flops | bytes accessed | tf_op | source)
XLA Modules:
  0.0 91.5 jit_solution(143786514412392632)
XLA Ops:
  0.6 88.7 %shard_map.94 = (f32[512,640]{1,0:T(8,128)S(1)}, f32[512,640]{1,0:T(8,128)S(1)}, f32[640,512]{1,0:T(8,128)S(1)}) custom-call(bf16[4,32,2048]{2,1,0:T(8,128)(2,1)} %tokens.1, bf16[4,32,2048]{2,1,0:T(8,128)(2,1)} %cotangent.1, s32[4,2,32]{2,1,0:T(2,128)} %bitcast.15, f32[4,2,32]{2,1,0:T(2,128)} %bitcast.16, bf16[2048,640]{1,0:T(8,128)(2,1)} %bitcast.12, ...), custom_call_target="tpu_custom_call" | custom-call | tf_op jit(solution)/shard_map/pallas_call | solution.py:615
  89.4 1.9 %shard_map.95 = (f32[512,640]{1,0:T(8,128)}, f32[512,640]{1,0:T(8,128)}, f32[640,512]{1,0:T(8,128)}) custom-call(f32[512,640]{1,0:T(8,128)S(1)} %get-tuple-element.9.refs_0_, f32[512,640]{1,0:T(8,128)S(1)} %get-tuple-element.10.refs_1_, f32[640,512]{1,0:T(8,128)S(1)} %get-tuple-element.11.refs_2_), custom_call_target="tpu_custom_call" | custom-call | tf_op jit(solution)/shard_map/pallas_call | solution.py:665

commit v5 on v4

--- a/solution.py
+++ b/solution.py
@@ -483,6 +483,10 @@
             def _():
                 forward_back(i - 2)
 
+            @pl.when((i >= 1) & (i < n_dp))
+            def _():
+                early_take(i)
+
         loop(batches + 1, backward)
 
     @pl.when(section == 1)
@@ -555,14 +559,18 @@
             grad_up[...] += up_part
             grad_down[...] += down_part
 
-    loop(n_dp, early_take, 1)
-    add_up(0)
-
-    @pl.when(section == 0)
-    def _():
-        forward_back(batches - 1)
-
-    loop(batches, add_up, 1)
+    @pl.when(section == 1)
+    def _():
+        loop(n_dp, early_take, 1)
+
+    def finish(b):
+        add_up(b)
+
+        @pl.when((section == 0) & (b == 1))
+        def _():
+            forward_back(batches - 1)
+
+    loop(batches, finish)
 
     def sent(b):
         exchanged(out_a, in_a, send_a, recv_a, b).wait_send()

time: 91.6 us -> 91.2 us (level)
  no operation moved by 1% of the time
where the time goes in v5:
time: 91.2 us; the launch traced here: 91.1 us
  Pallas kernels  90.5 us (99%)
    pallas_call x1, Pallas kernels, shards(): pl.pallas_call(functools.partial(kernel, (batches, tokens_b, slots, cap,...  88.5 us
    pallas_call x1, Pallas kernels, shards(): pl.pallas_call(hand_over, out_shape=[pltpu.HBM(out.shape, out.dtype) for...  1.95 us

profile of v5, /device:TPU:0, one launch (start us, length us, event | category | flops | bytes accessed | tf_op | source)
XLA Modules:
  0.0 91.1 jit_solution(15440776073735958712)
XLA Ops:
  0.6 88.5 %shard_map.94 = (f32[512,640]{1,0:T(8,128)S(1)}, f32[512,640]{1,0:T(8,128)S(1)}, f32[640,512]{1,0:T(8,128)S(1)}) custom-call(bf16[4,32,2048]{2,1,0:T(8,128)(2,1)} %tokens.1, bf16[4,32,2048]{2,1,0:T(8,128)(2,1)} %cotangent.1, s32[4,2,32]{2,1,0:T(2,128)} %bitcast.15, f32[4,2,32]{2,1,0:T(2,128)} %bitcast.16, bf16[2048,640]{1,0:T(8,128)(2,1)} %bitcast.12, ...), custom_call_target="tpu_custom_call" | custom-call | tf_op jit(solution)/shard_map/pallas_call | solution.py:623
  89.2 1.9 %shard_map.95 = (f32[512,640]{1,0:T(8,128)}, f32[512,640]{1,0:T(8,128)}, f32[640,512]{1,0:T(8,128)}) custom-call(f32[512,640]{1,0:T(8,128)S(1)} %get-tuple-element.9.refs_0_, f32[512,640]{1,0:T(8,128)S(1)} %get-tuple-element.10.refs_1_, f32[640,512]{1,0:T(8,128)S(1)} %get-tuple-element.11.refs_2_), custom_call_target="tpu_custom_call" | custom-call | tf_op jit(solution)/shard_map/pallas_call | solution.py:673

commit v6 on v5

--- a/solution.py
+++ b/solution.py
@@ -172,7 +172,7 @@
         )
 
     def share_part(source, into, which, b):
-        for q in range(1, n_dp):
+        for q in sorted(range(1, n_dp), key=lambda q: -min(q, n_dp - q)):
             lanes = pl.ds(pl.multiple_of(dp_at(q) * part, part), part)
             to_dp(source.at[b, :, lanes], into, which, b, q, dp_at(q)).start()
 

time: 91.2 us -> 91.2 us (level)
  no operation moved by 1% of the time
where the time goes in v6:
time: 91.2 us; the launch traced here: 91.1 us
  Pallas kernels  90.5 us (99%)
    pallas_call x1, Pallas kernels, shards(): pl.pallas_call(functools.partial(kernel, (batches, tokens_b, slots, cap,...  88.5 us
    pallas_call x1, Pallas kernels, shards(): pl.pallas_call(hand_over, out_shape=[pltpu.HBM(out.shape, out.dtype) for...  1.95 us

profile of v6, /device:TPU:0, one launch (start us, length us, event | category | flops | bytes accessed | tf_op | source)
XLA Modules:
  0.0 91.1 jit_solution(8690956172337952880)
XLA Ops:
  0.6 88.5 %shard_map.94 = (f32[512,640]{1,0:T(8,128)S(1)}, f32[512,640]{1,0:T(8,128)S(1)}, f32[640,512]{1,0:T(8,128)S(1)}) custom-call(bf16[4,32,2048]{2,1,0:T(8,128)(2,1)} %tokens.1, bf16[4,32,2048]{2,1,0:T(8,128)(2,1)} %cotangent.1, s32[4,2,32]{2,1,0:T(2,128)} %bitcast.15, f32[4,2,32]{2,1,0:T(2,128)} %bitcast.16, bf16[2048,640]{1,0:T(8,128)(2,1)} %bitcast.12, ...), custom_call_target="tpu_custom_call" | custom-call | tf_op jit(solution)/shard_map/pallas_call | solution.py:623
  89.2 1.9 %shard_map.95 = (f32[512,640]{1,0:T(8,128)}, f32[512,640]{1,0:T(8,128)}, f32[640,512]{1,0:T(8,128)}) custom-call(f32[512,640]{1,0:T(8,128)S(1)} %get-tuple-element.9.refs_0_, f32[512,640]{1,0:T(8,128)S(1)} %get-tuple-element.10.refs_1_, f32[640,512]{1,0:T(8,128)S(1)} %get-tuple-element.11.refs_2_), custom_call_target="tpu_custom_call" | custom-call | tf_op jit(solution)/shard_map/pallas_call | solution.py:673
